TPU v7x, 32 devices: a whole 2x2x4 slice. The times are simulated.
32 devices in a mesh: groups: 2 (over y), side: 4 (over z), dev: 4 (over x, core).
Axes of the slice: x: 2, y: 2, z: 4, core: 2. Of those that a mesh axis runs over, the one named last changes fastest.
Arguments:
- tokens: bfloat16 [128, 7168], P(('groups', 'side', 'dev')), parts along dimension 0, may hold values from -6 to 6
- routes: int32 [128, 4], P(('groups', 'side', 'dev')), parts along dimension 0, may hold values from 0 to 7, all different within a row; in each aligned block of 4 rows (0 to 3, 4 to 7, ...) at most 3 rows name the same one
- gate_weights: bfloat16 [128, 4], P(('groups', 'side', 'dev')), parts along dimension 0, may hold values from 0.049804688 to 1
- experts_in: bfloat16 [8, 2, 7168, 2048], P('side', None, None, 'dev'), may hold values from -0.0625 to 0.0625
- experts_out: bfloat16 [8, 2048, 7168], P('side', 'dev'), may hold values from -0.125 to 0.125
- query_latent: bfloat16 [64, 128, 512], P(('groups', 'side', 'dev')), parts along dimension 0, may hold values from -8 to 8
- query_rope: bfloat16 [64, 64, 128], P(('groups', 'side', 'dev')), parts along dimension 0, may hold values from -8 to 8
- cache_latent: bfloat16 [64, 512, 512], P(('groups', 'side', 'dev')), parts along dimension 0, may hold values from -8 to 8
- cache_rope: bfloat16 [64, 64, 512], P(('groups', 'side', 'dev')), parts along dimension 0, may hold values from -8 to 8
- lengths: int32 [64], P(('groups', 'side', 'dev')), parts along dimension 0, may hold values from 64 to 512, as said below
Outputs:
- routed_out: bfloat16 [128, 7168], P(('groups', 'side', 'dev')), parts along dimension 0
- attended: bfloat16 [64, 128, 512], P(('groups', 'side', 'dev')), parts along dimension 0
There are 2 independent parts, one for each index of `groups`. A program takes and returns all parts, laid end to end along the dimension named above; an argument that names none is the same for every part. Nothing has to cross between parts.
Inputs may be any that keep to these rules, and one draw needn't show every extreme that they name: `routes`: each row names 4 different experts. Among the 4 rows of one device no expert is named more than 3 times, and in every draw some device names some expert exactly 3 times. `lengths`: of every device's 2 requests one holds exactly 512 positions.
All inputs are finite; a program needn't handle non-finite values.
Results may differ from a plain program's by a relative error of at most 0.012.
Values may be sent and summed in bfloat16 or wider, within the bound.
No kernel may reach another device: no remote copies, remote signals or barrier semaphores. Data moves between devices by JAX's collectives and lax.ppermute only.
A program may use at most 128 MiB of HBM per device.

v0:
```python
import jax
import jax.numpy as jnp
from jax import lax
from jax.sharding import PartitionSpec as P

SCORE_SCALE = 192.0 ** (-0.5)


def routing_tables(routes, gate_weights, experts, capacity):
    flattened = routes.reshape(-1)
    member = (flattened[:, None] == jnp.arange(experts, dtype=jnp.int32)[None, :]).astype(jnp.int32)
    before = jnp.cumsum(member, axis=0) - member
    placed = flattened * capacity + jnp.sum(before * member, axis=1)
    onehot = placed[:, None] == jnp.arange(experts * capacity, dtype=jnp.int32)[None, :]
    onehot = onehot.reshape(routes.shape[0], routes.shape[1], experts * capacity)
    spread = jnp.sum(onehot.astype(jnp.float32), axis=1).astype(jnp.bfloat16)
    mixing = jnp.sum(jnp.where(onehot, gate_weights.astype(jnp.float32)[:, :, None], 0.0), axis=1)
    return (spread, mixing)


def expand(rows_in, experts_in):
    gate_up = jnp.einsum(
        "secd,egdh->secgh", rows_in, experts_in, preferred_element_type=jnp.float32
    )
    return (jax.nn.silu(gate_up[:, :, :, 0]) * gate_up[:, :, :, 1]).astype(jnp.bfloat16)


def attend(query_latent, query_rope, cache_latent, cache_rope, lengths):
    scores = jnp.einsum(
        "rhc,rpc->rhp", query_latent, cache_latent, preferred_element_type=jnp.float32
    )
    scores = (
        scores
        + jnp.einsum("rch,rcp->rhp", query_rope, cache_rope, preferred_element_type=jnp.float32)
    ) * SCORE_SCALE
    inside = (
        jnp.arange(cache_latent.shape[1], dtype=jnp.int32)[None, None, :] < lengths[:, None, None]
    )
    scores = jnp.where(inside, scores, -jnp.inf)
    highest = jnp.max(scores, axis=2, keepdims=True)
    shifted = jnp.exp(scores - highest)
    probability = (shifted / jnp.sum(shifted, axis=2, keepdims=True)).astype(jnp.bfloat16)
    return jnp.einsum(
        "rhp,rpc->rhc", probability, cache_latent, preferred_element_type=jnp.float32
    ).astype(jnp.bfloat16)


def shards(
    tokens,
    routes,
    gate_weights,
    experts_in,
    experts_out,
    query_latent,
    query_rope,
    cache_latent,
    cache_rope,
    lengths,
):
    side_count = lax.axis_size("side")
    node_experts = experts_in.shape[0]
    experts = node_experts * side_count
    tok_rows = tokens.shape[0]
    chosen = routes.shape[1]
    capacity = 3 * tok_rows * chosen // (2 * experts)
    width = tokens.shape[1]
    spread, mixing = routing_tables(routes, gate_weights, experts, capacity)
    outgoing = jnp.einsum("tj,td->jd", spread, tokens, preferred_element_type=jnp.float32).astype(
        jnp.bfloat16
    )
    outgoing = outgoing.reshape(side_count, node_experts, capacity, width)
    slot_weights = jnp.transpose(
        mixing.reshape(tok_rows, side_count, node_experts, capacity), (1, 2, 3, 0)
    ).astype(jnp.bfloat16)
    arrived_rows, arrived_weights = (
        lax.all_to_all(outgoing, "side", split_axis=0, concat_axis=0, tiled=True),
        lax.all_to_all(slot_weights, "side", split_axis=0, concat_axis=0, tiled=True),
    )
    rows_piece, weight_piece = lax.all_gather(
        (arrived_rows, arrived_weights), "dev", axis=0, tiled=True
    )
    count = rows_piece.shape[0] // side_count
    hidden = expand(rows_piece, experts_in)
    down = jnp.einsum("aech,ehd->aecd", hidden, experts_out, preferred_element_type=jnp.float32)
    terms = jnp.einsum(
        "aect,aecd->atd", weight_piece.astype(jnp.float32), down, precision=lax.Precision.HIGHEST
    )
    terms = terms.reshape(count, side_count, tok_rows, width)
    parts_all = jnp.transpose(terms, (1, 0, 2, 3)).astype(jnp.bfloat16)
    summed = lax.psum_scatter(
        parts_all.astype(jnp.float32).astype(jnp.bfloat16), "dev", scatter_dimension=1, tiled=True
    ).astype(jnp.float32)
    node_sum = summed.reshape(side_count, tok_rows, width).astype(jnp.bfloat16)
    returned = lax.all_to_all(node_sum, "side", split_axis=0, concat_axis=0, tiled=True)
    routed_out = jnp.sum(returned, axis=0, dtype=jnp.float32).astype(jnp.bfloat16)
    attended = attend(query_latent, query_rope, cache_latent, cache_rope, lengths)
    return (routed_out, attended)


def solution(mesh):
    return jax.shard_map(
        shards,
        mesh=mesh,
        in_specs=(
            P(("groups", "side", "dev"), None),
            P(("groups", "side", "dev"), None),
            P(("groups", "side", "dev"), None),
            P("side", None, None, "dev"),
            P("side", "dev", None),
            P(("groups", "side", "dev"), None, None),
            P(("groups", "side", "dev"), None, None),
            P(("groups", "side", "dev"), None, None),
            P(("groups", "side", "dev"), None, None),
            P(("groups", "side", "dev")),
        ),
        out_specs=(P(("groups", "side", "dev"), None), P(("groups", "side", "dev"), None, None)),
        check_vma=False,
    )
```

profile of v0, /device:TPU:0, one launch (start us, length us, event | category | flops | bytes accessed | tf_op | source)
XLA Modules:
  0.0 126.3 jit_solution(11262036179693291630)
XLA Ops:
  7.2 0.0 copy-start
  7.2 0.0 copy-start.7
  7.2 0.0 copy-start.4
  7.2 0.0 copy-start.3
  7.2 0.0 all-gather.2.cloned.1.call-start
  7.3 0.8 eq.29
  8.1 0.1 fusion.25
  8.2 0.2 select_reduce_fusion.1
  8.4 0.1 reduce_sum.51
  8.5 0.7 multiply_add_fusion
  9.2 0.7 convert_element_type.53
  9.9 0.1 convert_reduce_fusion
  10.0 1.1 convolution_convert_fusion
  11.1 0.2 reshape.56
  11.3 0.3 copy.30
  11.6 16.9 %all_to_all.15 = bf16[4,2,3,7168]{3,1,2,0:T(2,128)(2,1)} all-to-all(bf16[4,2,3,7168]{3,1,2,0:T(2,128)(2,1)S(1)} %copy.30), channel_id=1, replica_groups=mesh['groups'=2,'side'=4,'dev'=4] {'side'}, dimensions={0} | all-to-all | bytes 688128 | tf_op jit(solution)/shard_map/all_to_all | solution.py:76
  28.4 0.0 all-gather.2.cloned.1.call-update
  28.5 0.1 convert_element_type.55
  28.6 0.7 copy.29
  29.3 3.2 %all-to-all-start = ((bf16[4,2,3,4]{3,1,2,0:T(2,128)(2,1)}), bf16[4,2,3,4]{3,1,2,0:T(2,128)(2,1)S(1)}, u32[]{:S(2)}, u32[]{:S(2)}) async-start(bf16[4,2,3,4]{3,1,2,0:T(2,128)(2,1)} %copy.29), calls=%async_computation | async-start | bytes 12288 | tf_op jit(solution)/shard_map/all_to_all | solution.py:77
  32.5 0.0 all-reduce.3.cloned.1.call-start
  32.6 0.0 copy-done.4
  32.6 0.0 slice-start
  32.6 1.1 fusion.30
  33.7 0.0 copy-done.7
  33.7 0.6 dynamic-slice
  34.3 3.8 %all-to-all-done = bf16[4,2,3,4]{3,1,2,0:T(2,128)(2,1)S(1)} async-done(((bf16[4,2,3,4]{3,1,2,0:T(2,128)(2,1)}), bf16[4,2,3,4]{3,1,2,0:T(2,128)(2,1)S(1)}, u32[]{:S(2)}, u32[]{:S(2)}) %all-to-all-start) | async-done | bytes 224 | tf_op jit(solution)/shard_map/all_to_all | solution.py:77
  38.1 5.7 %all_gather.6 = bf16[16,2,3,4]{3,1,2,0:T(2,128)(2,1)} all-gather(bf16[4,2,3,4]{3,1,2,0:T(2,128)(2,1)S(1)} %all-to-all-done), channel_id=1, replica_groups=mesh['groups'=2,'side'=4,'dev'=4] {'dev'}, dimensions={0}, use_global_device_ids=true | all-gather | bytes 960 | tf_op jit(solution)/shard_map/all_gather | solution.py:79
  43.8 2.6 %all-gather.2.cloned.1.call-done = bf16[16,2,3,7168]{3,1,2,0:T(2,128)(2,1)} async-done(((bf16[4,2,3,7168]{3,1,2,0:T(2,128)(2,1)}), bf16[16,2,3,7168]{3,1,2,0:T(2,128)(2,1)}) %all-gather.2.cloned.1.call-update) | async-done | bytes 1376272 | tf_op jit(solution)/shard_map/all_gather | solution.py:79
  46.4 12.0 %fusion.15 = f32[16,2,3,2,512]{4,0,3,2,1:T(8,128)S(1)} fusion(bf16[2,2,7168,512]{3,2,1,0:T(8,128)(2,1)} %param.13, bf16[16,2,3,7168,1]{3,1,2,0,4:T(2,128)(2,1)} %bitcast.57), kind=kOutput, calls=%fused_computation.17 | convolution fusion | flops 1409286144 | bytes 31129600 | tf_op jit(solution)/shard_map/secd,egdh->secgh/dot_general | solution.py:22
  58.4 0.2 slice-done.2
  58.7 1.2 slice-done.3
  59.8 2.6 %fusion.5 = f32[16,2,3,7168]{3,0,2,1:T(8,128)S(1)} fusion(bf16[2,512,7168]{2,1,0:T(8,128)(2,1)S(1)} %bitcast.56, f32[16,2,3,2,512]{4,0,3,2,1:T(8,128)S(1)} %fusion.15), kind=kOutput, calls=%fused_computation.5 | convolution fusion | flops 704937984 | bytes 17825792 | tf_op jit(solution)/shard_map/aech,ehd->aecd/dot_general | solution.py:84
  62.5 0.0 copy-done.5
  62.5 0.0 copy-start.6
  62.5 0.0 copy-start.2
  62.5 6.0 %fusion.8 = bf16[16,4,7168]{2,1,0:T(4,128)(2,1)} fusion(bf16[16,2,3,4]{3,1,2,0:T(2,128)(2,1)S(1)} %copy-done.5, f32[16,2,3,7168]{3,0,2,1:T(8,128)S(1)} %fusion.5), kind=kOutput, calls=%fused_computation.7 | convolution fusion | flops 33488896 | bytes 3670784 | tf_op jit(solution)/shard_map/aect,aecd->atd/dot_general | solution.py:85
  68.6 0.0 all-reduce.3.cloned.1.call-update
  68.6 0.1 iota_compare_fusion.2
  68.7 0.0 copy-done.1
  68.7 0.5 fusion.13
  69.2 34.8 %all-reduce.3.cloned.1.call-done = bf16[4,4,4,7168]{3,2,0,1:T(4,128)(2,1)} async-done(((bf16[4,4,4,7168]{3,2,0,1:T(4,128)(2,1)}), bf16[4,4,4,7168]{3,2,0,1:T(4,128)(2,1)}) %all-reduce.3.cloned.1.call-update) | async-done | bytes 917520
  104.0 2.4 %dynamic-slice_bitcast_fusion = bf16[4,4,7168]{2,1,0:T(4,128)(2,1)} fusion(bf16[4,4,4,7168]{3,2,0,1:T(4,128)(2,1)} %all-reduce.3.cloned.1.call-done, u32[]{:T(128)} %bitcast.18), kind=kLoop, calls=%fused_computation.20 | loop fusion | bytes 458756 | tf_op jit(solution)/shard_map/convert_element_type | solution.py:93
  106.3 4.6 %all-to-all-start.2 = ((bf16[4,4,7168]{2,1,0:T(4,128)(2,1)}), bf16[4,4,7168]{2,1,0:T(4,128)(2,1)S(1)}, u32[]{:S(2)}, u32[]{:S(2)}) async-start(bf16[4,4,7168]{2,1,0:T(4,128)(2,1)} %dynamic-slice_bitcast_fusion), calls=%async_computation.2 | async-start | bytes 458752 | tf_op jit(solution)/shard_map/all_to_all | solution.py:94
  110.9 0.2 fusion.29
  111.2 1.3 %convolution_convert_fusion.1 = bf16[2,128,512]{2,1,0:T(8,128)(2,1)} fusion(bf16[2,512,512]{2,1,0:T(8,128)(2,1)S(1)} %copy-done, f32[2,128]{1,0:T(2,128)S(1)} %fusion.29, f32[2,128,512]{2,1,0:T(8,128)S(1)} %fusion.13), kind=kOutput, calls=%fused_computation.16 | convolution fusion | flops 134742784 | bytes 1836032 | tf_op jit(solution)/shard_map/rhp,rpc->rhc/dot_general | solution.py:43
  112.4 6.2 %all-to-all-done.2 = bf16[4,4,7168]{2,1,0:T(4,128)(2,1)S(1)} async-done(((bf16[4,4,7168]{2,1,0:T(4,128)(2,1)}), bf16[4,4,7168]{2,1,0:T(4,128)(2,1)S(1)}, u32[]{:S(2)}, u32[]{:S(2)}) %all-to-all-start.2) | async-done | bytes 229408 | tf_op jit(solution)/shard_map/all_to_all | solution.py:94
  118.7 0.7 reduce_sum.54
  (13 shorter events, 0.1 us)
Async XLA Ops:
  7.2 61.5 %copy-start = (bf16[2,512,512]{2,1,0:T(8,128)(2,1)S(1)}, bf16[2,512,512]{2,1,0:T(8,128)(2,1)}, u32[]{:S(2)}) copy-start(bf16[2,512,512]{2,1,0:T(8,128)(2,1)} %param.17) | copy-start | bytes 3145732
  7.2 26.6 %copy-start.7 = (u32[32]{0:T(128)S(1)}, u32[32]{0:T(128)}, u32[]{:S(2)}) copy-start(u32[32]{0:T(128)} %constant.31) | copy-start | bytes 388
  7.2 25.4 %copy-start.4 = (bf16[2,64,128]{2,1,0:T(8,128)(2,1)S(1)}, bf16[2,64,128]{2,1,0:T(8,128)(2,1)}, u32[]{:S(2)}) copy-start(bf16[2,64,128]{2,1,0:T(8,128)(2,1)} %param.16) | copy-start | bytes 98308
  7.2 25.4 %copy-start.3 = (bf16[2,64,512]{2,1,0:T(8,128)(2,1)S(1)}, bf16[2,64,512]{2,1,0:T(8,128)(2,1)}, u32[]{:S(2)}) copy-start(bf16[2,64,512]{2,1,0:T(8,128)(2,1)} %param.18) | copy-start | bytes 393220
  7.2 39.2 %all-gather.2.cloned.1.call-start = ((), (), s32[]{:S(2)}) async-start(), calls=%async_computation.3 | async-start | bytes 1720320 | tf_op jit(solution)/shard_map/all_gather | solution.py:79
  29.3 8.8 %all-to-all-start = ((bf16[4,2,3,4]{3,1,2,0:T(2,128)(2,1)}), bf16[4,2,3,4]{3,1,2,0:T(2,128)(2,1)S(1)}, u32[]{:S(2)}, u32[]{:S(2)}) async-start(bf16[4,2,3,4]{3,1,2,0:T(2,128)(2,1)} %copy.29), calls=%async_computation | async-start | bytes 12288 | tf_op jit(solution)/shard_map/all_to_all | solution.py:77
  32.5 71.4 %all-reduce.3.cloned.1.call-start = ((), (), s32[]{:S(2)}) async-start(), calls=%async_computation.4 | async-start | bytes 1835008
  32.6 25.8 %slice-start = ((s8[14680064]{0:T(1024)(128)(4,1)}), s8[2097152]{0:T(1024)(128)(4,1)S(1)}, s32[]{:S(2)}) async-start(s8[14680064]{0:T(1024)(128)(4,1)} %bitcast.55), calls=%async_computation.5 | async-start | bytes 4194304
  46.4 12.0 %slice-start.1 = ((s8[14680064]{0:T(1024)(128)(4,1)}), s8[4194304]{0:T(1024)(128)(4,1)S(1)}, s32[]{:S(2)}) async-start(s8[14680064]{0:T(1024)(128)(4,1)} %bitcast.55), calls=%async_computation.6 | async-start | bytes 8388608
  46.4 12.2 %slice-start.2 = ((s8[14680064]{0:T(1024)(128)(4,1)}), s8[4194304]{0:T(1024)(128)(4,1)S(1)}, s32[]{:S(2)}) async-start(s8[14680064]{0:T(1024)(128)(4,1)} %bitcast.55), calls=%async_computation.7 | async-start | bytes 8388608
  46.4 13.4 %slice-start.3 = ((s8[14680064]{0:T(1024)(128)(4,1)}), s8[4194304]{0:T(1024)(128)(4,1)S(1)}, s32[]{:S(2)}) async-start(s8[14680064]{0:T(1024)(128)(4,1)} %bitcast.55), calls=%async_computation.8 | async-start | bytes 8388608
  59.8 2.6 %copy-start.5 = (bf16[16,2,3,4]{3,1,2,0:T(2,128)(2,1)S(1)}, bf16[16,2,3,4]{3,1,2,0:T(2,128)(2,1)}, u32[]{:S(2)}) copy-start(bf16[16,2,3,4]{3,1,2,0:T(2,128)(2,1)} %all_gather.6) | copy-start | bytes 2308
  62.5 6.1 %copy-start.6 = (s32[2]{0:T(128)S(1)}, s32[2]{0:T(128)}, u32[]{:S(2)}) copy-start(s32[2]{0:T(128)} %param.19) | copy-start | bytes 28
  62.5 6.2 %copy-start.1 = (f32[2,128,512]{2,1,0:T(8,128)S(1)}, f32[2,128,512]{2,1,0:T(8,128)}, u32[]{:S(2)}) copy-start(f32[2,128,512]{2,1,0:T(8,128)} %fusion.30) | copy-start | bytes 1572868
  62.5 6.2 %copy-start.2 = (bf16[2,128,512]{2,1,0:T(8,128)(2,1)S(1)}, bf16[2,128,512]{2,1,0:T(8,128)(2,1)}, u32[]{:S(2)}) copy-start(bf16[2,128,512]{2,1,0:T(8,128)(2,1)} %param.15) | copy-start | bytes 786436
  106.3 12.3 %all-to-all-start.2 = ((bf16[4,4,7168]{2,1,0:T(4,128)(2,1)}), bf16[4,4,7168]{2,1,0:T(4,128)(2,1)S(1)}, u32[]{:S(2)}, u32[]{:S(2)}) async-start(bf16[4,4,7168]{2,1,0:T(4,128)(2,1)} %dynamic-slice_bitcast_fusion), calls=%async_computation.2 | async-start | bytes 458752 | tf_op jit(solution)/shard_map/all_to_all | solution.py:94
Sparse Core Ops, SparseCore 0:
  28.6 17.7 all-gather.1
  68.7 35.2 all-reduce.2
where the time goes:
time: 127 us; the launch traced here: 126 us
  waiting for transfers between devices  47.5 us (37%)
  matrix products  24.6 us (19%)
  blocking collectives  22.6 us (18%)
  between operations  14.2 us (11%)
  starting transfers between devices  7.93 us (6%)
  local copies, waits for them, and re-layouts  6.69 us (5%)
  other arithmetic  2.81 us (2%)
    unnamed x3, waiting for transfers between devices  34.9 us
    all_to_all x1, blocking collectives, shards(): lax.all_to_all(outgoing, 'side', split_axis=0, concat_axis=0, tiled=True)  16.9 us
    dot_general x1, matrix products, expand(): jnp.einsum('secd,egdh->secgh', rows_in, experts_in, preferred_element_typ...  12 us
    all_to_all x1, waiting for transfers between devices, shards(): lax.all_to_all(node_sum, 'side', split_axis=0, concat_axis=0, tiled=True)  6.24 us
    dot_general x1, matrix products, shards(): jnp.einsum('aect,aecd->atd', weight_piece.astype(jnp.float32), down, prec...  6.04 us
    all_gather x1, blocking collectives, shards(): lax.all_gather((arrived_rows, arrived_weights), 'dev', axis=0, tiled=True)  5.72 us
    all_to_all x1, starting transfers between devices, shards(): lax.all_to_all(node_sum, 'side', split_axis=0, concat_axis=0, tiled=True)  4.6 us
    all_to_all x1, waiting for transfers between devices, shards(): lax.all_to_all(slot_weights, 'side', split_axis=0, concat_axis=0, tiled=T...  3.8 us
  transfers between devices with their start and end apart: 4, of which 4 were waited for; matrix products, arithmetic and copies ran while one was open for 4% of the time, Pallas kernels for 0%

commit v1 on v0

v1 whole, which is shorter than its diff:
```python
import functools

import jax
import jax.numpy as jnp
from jax import lax
from jax.experimental import pallas as pl
from jax.experimental.pallas import tpu as pltpu
from jax.sharding import PartitionSpec as P

SCORE_SCALE = 192.0 ** (-0.5)
BF16 = jnp.bfloat16
F32 = jnp.float32
LANES = 128


def swap(x, side_bits, dev_bits):
    side, dev = lax.axis_size("side"), lax.axis_size("dev")
    if side_bits == 0:
        return lax.ppermute(x, "dev", [(i, i ^ dev_bits) for i in range(dev)])
    if dev_bits == 0:
        return lax.ppermute(x, "side", [(i, i ^ side_bits) for i in range(side)])
    pairs = [(i, i ^ (side_bits * dev + dev_bits)) for i in range(side * dev)]
    return lax.ppermute(x, ("side", "dev"), pairs)


def pack_kernel(tokens, routes, gates, out):
    width = tokens.shape[1]
    out[:, :width] = tokens[...]
    pad = out.shape[1] - width
    lane = lax.broadcasted_iota(jnp.int32, (tokens.shape[0], pad), 1)
    total = jnp.zeros((tokens.shape[0], pad), F32)
    gate = gates[...].astype(F32)
    for k in range(routes.shape[1]):
        total = total + jnp.where(routes[:, k : k + 1] == lane, gate[:, k : k + 1], 0.0)
    out[:, width:] = total.astype(BF16)


def pack(tokens, routes, gates, experts):
    rows, width = tokens.shape
    pad = -(-experts // LANES) * LANES
    return pl.pallas_call(
        pack_kernel,
        out_shape=jax.ShapeDtypeStruct((rows, width + pad), BF16),
        compiler_params=pltpu.CompilerParams(vmem_limit_bytes=2 * 1024 * 1024),
        name="pack",
    )(tokens, routes, gates)


def chunks_of(width):
    step = 1024 if width % 1024 == 0 else width
    return step, width // step


def fetch_copies(e, w_in, held, sems):
    step, count = chunks_of(w_in.shape[2])
    return [
        pltpu.make_async_copy(
            w_in.at[e, g, pl.ds(i * step, step)], held.at[g, pl.ds(i * step, step)], sems.at[g * count + i]
        )
        for i in range(count)
        for g in range(2)
    ]


def fetch_kernel(e, w_in, held, sems):
    copies = fetch_copies(e, w_in, held, sems)
    for copy in copies:
        copy.start()
    for copy in copies:
        copy.wait()


def attend_kernel(
    e, lengths, w_in, queries, rope_queries, latents, ropes, held, attended, q, qr, c, cr, sems, own_sems
):
    own = [
        pltpu.make_async_copy(source, target, own_sems.at[i])
        for i, (source, target) in enumerate(((queries, q), (rope_queries, qr), (latents, c), (ropes, cr)))
    ]
    copies = fetch_copies(e, w_in, held, sems)
    for copy in own + copies:
        copy.start()
    for copy in own:
        copy.wait()
    for r in range(q.shape[0]):
        latent = c[r]
        scores = lax.dot_general(
            q[r], latent, (((1,), (1,)), ((), ())), preferred_element_type=F32
        ) + lax.dot_general(qr[r], cr[r], (((0,), (0,)), ((), ())), preferred_element_type=F32)
        scores = scores * SCORE_SCALE
        place = lax.broadcasted_iota(jnp.int32, scores.shape, 1)
        scores = jnp.where(place < lengths[r], scores, -jnp.inf)
        shifted = jnp.exp(scores - jnp.max(scores, axis=1, keepdims=True))
        shares = (shifted / jnp.sum(shifted, axis=1, keepdims=True)).astype(BF16)
        attended[r] = jnp.dot(shares, latent, preferred_element_type=F32).astype(BF16)
    for copy in copies:
        copy.wait()


def fetch(e, w_in, attention=None):
    _, _, width, block = w_in.shape
    sems = pltpu.SemaphoreType.DMA((2 * chunks_of(width)[1],))
    held = pltpu.VMEM((2, width, block), BF16)
    anywhere, vmem = pl.BlockSpec(memory_space=pltpu.HBM), pl.BlockSpec(memory_space=pltpu.VMEM)
    cost = pl.CostEstimate(flops=0, bytes_accessed=4 * width * block, transcendentals=0)
    if attention is None:
        return pl.pallas_call(
            functools.partial(fetch_kernel, e),
            out_shape=held,
            in_specs=[anywhere],
            out_specs=vmem,
            scratch_shapes=[sems],
            compiler_params=pltpu.CompilerParams(vmem_limit_bytes=2 * 1024 * 1024),
            cost_estimate=cost,
            name="fetch",
        )(in_hbm(w_in))
    arrays, lengths = attention[:-1], attention[-1]
    return pl.pallas_call(
        functools.partial(attend_kernel, e),
        out_shape=(held, jax.ShapeDtypeStruct(arrays[0].shape, BF16)),
        in_specs=[pl.BlockSpec(memory_space=pltpu.SMEM)] + [anywhere] * 5,
        out_specs=(vmem, vmem),
        scratch_shapes=[pltpu.VMEM(x.shape, BF16) for x in arrays] + [sems, pltpu.SemaphoreType.DMA((4,))],
        compiler_params=pltpu.CompilerParams(vmem_limit_bytes=8 * 1024 * 1024),
        cost_estimate=cost,
        name="attend",
    )(lengths, in_hbm(w_in), *[in_hbm(x) for x in arrays])


def experts_kernel(pieces, count, *refs):
    parts, refs = refs[:pieces], refs[pieces:]
    w_in, w_out, outs = refs[:count], refs[count], refs[count + 1 : -4]
    rows, act, held, sems = refs[-4:]
    _, block, width = w_out.shape
    step, chunks = chunks_of(width)
    copies = [
        pltpu.make_async_copy(w_out.at[:, :, pl.ds(i * step, step)], held.at[:, :, pl.ds(i * step, step)], sems.at[i])
        for i in range(chunks)
    ]
    for copy in copies:
        copy.start()
    size = parts[0].shape[0]
    for i, part in enumerate(parts):
        rows[i * size : (i + 1) * size, :] = part[...]
    first = lax.axis_index("side") * count
    gates = rows[:, width:].astype(F32)
    lane = lax.broadcasted_iota(jnp.int32, gates.shape, 1)
    for e in range(count):
        gate = jnp.dot(rows[:, :width], w_in[e][0], preferred_element_type=F32)
        up = jnp.dot(rows[:, :width], w_in[e][1], preferred_element_type=F32)
        weight = jnp.sum(jnp.where(lane == first + e, gates, 0.0), axis=1, keepdims=True)
        value = gate / (1.0 + jnp.exp(-gate)) * up * weight
        act[:, e * block : (e + 1) * block] = value.astype(BF16)
    for i, copy in enumerate(copies):
        copy.wait()
        at = slice(i * step, (i + 1) * step)
        total = jnp.dot(act[:, :block], held[0, :, at], preferred_element_type=F32)
        for e in range(1, count):
            total = total + jnp.dot(
                act[:, e * block : (e + 1) * block], held[e, :, at], preferred_element_type=F32
            )
        total = total.astype(BF16)
        start = 0
        for out in outs:
            out[:, at] = total[start : start + out.shape[0]]
            start += out.shape[0]


def in_hbm(x):
    return pltpu.with_memory_space_constraint(x, pltpu.HBM)


def in_vmem(x):
    return pltpu.with_memory_space_constraint(x, pltpu.VMEM)


def run_experts(near, far, w_in, w_out):
    parts = [*near, *far]
    size, packed = parts[0].shape
    total = size * len(parts)
    count, block, width = w_out.shape
    outs = [pltpu.VMEM((size, width), BF16) for _ in near] + [pltpu.VMEM((size * len(far), width), BF16)]
    whole = pl.BlockSpec(memory_space=pltpu.VMEM)
    results = pl.pallas_call(
        functools.partial(experts_kernel, len(parts), count),
        out_shape=outs,
        in_specs=[whole] * (len(parts) + count) + [pl.BlockSpec(memory_space=pltpu.HBM)],
        out_specs=[whole] * len(outs),
        scratch_shapes=[
            pltpu.VMEM((total, packed), BF16),
            pltpu.VMEM((total, count * block), BF16),
            pltpu.VMEM(w_out.shape, BF16),
            pltpu.SemaphoreType.DMA((chunks_of(width)[1],)),
        ],
        compiler_params=pltpu.CompilerParams(vmem_limit_bytes=24 * 1024 * 1024),
        cost_estimate=pl.CostEstimate(
            flops=6 * total * count * width * block, bytes_accessed=6 * count * width * block, transcendentals=0
        ),
        name="experts",
    )(*[in_vmem(x) for x in parts], *[in_vmem(w) for w in w_in], in_hbm(w_out))
    return results[:-1], results[-1]


def add(*terms):
    total = terms[0].astype(F32)
    for term in terms[1:]:
        total = total + term.astype(F32)
    return total.astype(BF16)


def shards(
    tokens,
    routes,
    gate_weights,
    experts_in,
    experts_out,
    query_latent,
    query_rope,
    cache_latent,
    cache_rope,
    lengths,
):
    side, dev = lax.axis_size("side"), lax.axis_size("dev")
    chips = dev // 2
    count = tokens.shape[0]
    packed = pack(tokens, routes, gate_weights, experts_in.shape[0] * side)
    attention = (query_latent, query_rope, cache_latent, cache_rope, lengths)
    first, attended = fetch(0, experts_in, attention)
    along = [packed] + [swap(packed, k, 0) for k in range(1, side)]
    *along, first, attended = lax.optimization_barrier((*along, first, attended))
    along = jnp.concatenate(along)
    near = [along] + [swap(along, 0, 2 * k) for k in range(1, chips)]
    others = [fetch(e, experts_in) for e in range(1, experts_in.shape[0])]
    far = [swap(near[0], 0, 1)]
    near, others = lax.optimization_barrier((near, others))
    far += [swap(piece, 0, 1) for piece in near[1:]]
    weights = [first] + others
    near_part, far_part = run_experts(near, far, weights, experts_out)
    far_part = swap(far_part, 0, 1)
    size = side * count
    both = [add(part, far_part[k * size : (k + 1) * size]) for k, part in enumerate(near_part)]
    column = add(both[0], *[swap(both[k], 0, 2 * k) for k in range(1, chips)])
    routed_out = add(
        column[:count],
        *[swap(column[k * count : (k + 1) * count], k, 0) for k in range(1, side)],
    )
    return (routed_out, attended)


def solution(mesh):
    return jax.shard_map(
        shards,
        mesh=mesh,
        in_specs=(
            P(("groups", "side", "dev"), None),
            P(("groups", "side", "dev"), None),
            P(("groups", "side", "dev"), None),
            P("side", None, None, "dev"),
            P("side", "dev", None),
            P(("groups", "side", "dev"), None, None),
            P(("groups", "side", "dev"), None, None),
            P(("groups", "side", "dev"), None, None),
            P(("groups", "side", "dev"), None, None),
            P(("groups", "side", "dev")),
        ),
        out_specs=(P(("groups", "side", "dev"), None), P(("groups", "side", "dev"), None, None)),
        check_vma=False,
    )
```

time: 127 us -> 57.4 us (0.45)
  waiting for transfers between devices: 47.5 us -> 14.9 us
  matrix products: 24.6 us -> 0 us
  Pallas kernels: 0 us -> 24.2 us
  blocking collectives: 22.6 us -> 0 us
  between operations: 14.2 us -> 0.74 us
  starting transfers between devices: 7.93 us -> 13.6 us
  local copies, waits for them, and re-layouts: 6.69 us -> 2.9 us
  other arithmetic: 2.81 us -> 0.97 us
    unnamed x3 -> x0, waiting for transfers between devices: 34.9 us -> none
    dot_general x7 -> x0, matrix products: 24.6 us -> none  [the longest x1 12 us: expand(): jnp.einsum('secd,egdh->secgh', rows_in, experts_in, preferred_element_typ...]
    pallas_call x0 -> x4, Pallas kernels: none -> 24.2 us  [the longest x1 10.9 us: run_experts(): pl.pallas_call(functools.partial(experts_kernel, len(parts), count), out_...]
    all_to_all x1 -> x0, blocking collectives: 16.9 us -> none  [shards(): lax.all_to_all(outgoing, 'side', split_axis=0, concat_axis=0, tiled=True)]
    ppermute x0 -> x11, waiting for transfers between devices: none -> 14.9 us  [the longest x5 9.63 us: swap(): return lax.ppermute(x, 'dev', [(i, i ^ dev_bits) for i in range(dev)])]
    ppermute x0 -> x11, starting transfers between devices: none -> 13.6 us  [the longest x6 9.99 us: swap(): return lax.ppermute(x, 'side', [(i, i ^ side_bits) for i in range(side)])]
    all_to_all x2 -> x0, waiting for transfers between devices: 10 us -> none  [the longest x1 6.24 us: shards(): lax.all_to_all(node_sum, 'side', split_axis=0, concat_axis=0, tiled=True)]
    all_to_all x2 -> x0, starting transfers between devices: 7.85 us -> none  [the longest x1 4.6 us: shards(): lax.all_to_all(node_sum, 'side', split_axis=0, concat_axis=0, tiled=True)]
  transfers between devices with their start and end apart: 4 -> 11, of which waited for: 4 -> 6; matrix products, arithmetic and copies ran while one was open for 4% -> 0% of each run, Pallas kernels for 0% -> 23%
where the time goes in v1:
time: 57.4 us; the launch traced here: 57.2 us
  Pallas kernels  24.2 us (42%)
  waiting for transfers between devices  14.9 us (26%)
  starting transfers between devices  13.6 us (24%)
  local copies, waits for them, and re-layouts  2.9 us (5%)
  other arithmetic  0.97 us (2%)
  between operations  0.74 us (1%)
    pallas_call x1, Pallas kernels, run_experts(): pl.pallas_call(functools.partial(experts_kernel, len(parts), count), out_...  10.9 us
    ppermute x6, starting transfers between devices, swap(): return lax.ppermute(x, 'side', [(i, i ^ side_bits) for i in range(side)])  9.99 us
    ppermute x5, waiting for transfers between devices, swap(): return lax.ppermute(x, 'dev', [(i, i ^ dev_bits) for i in range(dev)])  9.63 us
    pallas_call x1, Pallas kernels, fetch(): pl.pallas_call(functools.partial(attend_kernel, e), out_shape=(held, jax....  7.94 us
    pallas_call x1, Pallas kernels, fetch(): pl.pallas_call(functools.partial(fetch_kernel, e), out_shape=held, in_spe...  5.31 us
    ppermute x6, waiting for transfers between devices, swap(): return lax.ppermute(x, 'side', [(i, i ^ side_bits) for i in range(side)])  5.23 us
    ppermute x5, starting transfers between devices, swap(): return lax.ppermute(x, 'dev', [(i, i ^ dev_bits) for i in range(dev)])  3.58 us
    unnamed x8, local copies, waits for them, and re-layouts  2.83 us
  transfers between devices with their start and end apart: 11, of which 6 were waited for; matrix products, arithmetic and copies ran while one was open for 0% of the time, Pallas kernels for 23%

profile of v1, /device:TPU:0, one launch (start us, length us, event | category | flops | bytes accessed | tf_op | source)
XLA Modules:
  0.0 57.2 jit_solution(5959622569224006711)
XLA Ops:
  0.6 0.0 copy-start
  0.6 0.8 %copy-done = bf16[4,7168]{1,0:T(4,128)(2,1)S(1)} copy-done((bf16[4,7168]{1,0:T(4,128)(2,1)S(1)}, bf16[4,7168]{1,0:T(4,128)(2,1)}, u32[]{:S(2)}) %copy-start) | copy-done | bytes 57368
  1.4 0.0 copy-start.1
  1.5 0.7 %copy-done.1 = s32[4,4]{1,0:T(4,128)S(1)} copy-done((s32[4,4]{1,0:T(4,128)S(1)}, s32[4,4]{1,0:T(4,128)}, u32[]{:S(2)}) %copy-start.1) | copy-done | bytes 88
  2.1 0.0 copy-start.2
  2.1 0.7 %copy-done.2 = bf16[4,4]{1,0:T(4,128)(2,1)S(1)} copy-done((bf16[4,4]{1,0:T(4,128)(2,1)S(1)}, bf16[4,4]{1,0:T(4,128)(2,1)}, u32[]{:S(2)}) %copy-start.2) | copy-done | bytes 56
  2.8 0.1 pack.1
  2.9 5.1 %collective-permute-start.2 = (bf16[4,7296]{1,0:T(4,128)(2,1)S(1)}, bf16[4,7296]{1,0:T(4,128)(2,1)S(1)}, u32[]{:S(2)}, u32[]{:S(2)}) collective-permute-start(bf16[4,7296]{1,0:T(4,128)(2,1)S(1)} %pack.1), channel_id=1, source_target_pairs={{0,12},{4,8},{8,4},{12,0},{1,13},{5,9},{9,5},{13,1},{2,14},{6,10},... | collective-permute-start | bytes 175112 | tf_op jit(solution)/shard_map/ppermute | solution.py:21
  8.0 0.0 collective-permute-start.1
  8.0 0.6 %collective-permute-start = (bf16[4,7296]{1,0:T(4,128)(2,1)S(1)}, bf16[4,7296]{1,0:T(4,128)(2,1)S(1)}, u32[]{:S(2)}, u32[]{:S(2)}) collective-permute-start(bf16[4,7296]{1,0:T(4,128)(2,1)S(1)} %pack.1), channel_id=1, source_target_pairs={{0,4},{4,0},{8,12},{12,8},{1,5},{5,1},{9,13},{13,9},{2,6},{6,2},{1... | collective-permute-start | bytes 175112 | tf_op jit(solution)/shard_map/ppermute | solution.py:21
  8.7 0.0 copy-start.3
  8.7 0.7 %copy-done.3 = s32[2]{0:T(128)S(1)} copy-done((s32[2]{0:T(128)S(1)}, s32[2]{0:T(128)}, u32[]{:S(2)}) %copy-start.3) | copy-done | bytes 32
  9.3 7.9 %attend.1 = (bf16[2,7168,512]{2,1,0:T(8,128)(2,1)S(1)}, bf16[2,128,512]{2,1,0:T(8,128)(2,1)}) custom-call(s32[2]{0:T(128)S(1)} %copy-done.3, bf16[2,2,7168,512]{3,2,1,0:T(8,128)(2,1)} %w_in.3, bf16[2,128,512]{2,1,0:T(8,128)(2,1)} %queries.1, bf16[2,64,128]{2,1,0:T(8,128)(2,1)} %rope_queries.1, bf16[2,512,512]{2,1,0:T(8,128)(2,1)} %latents.1, ...), custom_call_target="tpu_custom_call" | custom-call | bytes 14680064 | tf_op jit(solution)/shard_map/attend/pallas_call | solution.py:118
  17.3 0.0 collective-permute-done.2
  17.3 0.0 collective-permute-done.1
  17.3 0.0 collective-permute-done
  17.3 0.1 pad_maximum_fusion.refs_0_
  17.4 1.7 %collective-permute-start.3 = (bf16[16,7296]{1,0:T(8,128)(2,1)S(1)}, bf16[16,7296]{1,0:T(8,128)(2,1)S(1)}, u32[]{:S(2)}, u32[]{:S(2)}) collective-permute-start(bf16[16,7296]{1,0:T(8,128)(2,1)S(1)} %pad_maximum_fusion.refs_0_), channel_id=1, source_target_pairs={{0,2},{1,3},{2,0},{3,1},{4,6},{5,7},{6,4},{7,5},{8,10},{9,11},{10,... | collective-permute-start | bytes 700424 | tf_op jit(solution)/shard_map/ppermute | solution.py:19
  19.1 5.3 %fetch.1.refs_5_ = bf16[2,7168,512]{2,1,0:T(8,128)(2,1)S(1)} custom-call(bf16[2,2,7168,512]{3,2,1,0:T(8,128)(2,1)} %w_in.3), custom_call_target="tpu_custom_call" | custom-call | bytes 14680064 | tf_op jit(solution)/shard_map/fetch/pallas_call | solution.py:107
  24.5 0.1 collective-permute-start.4
  24.5 0.0 collective-permute-done.3.refs_1_
  24.5 0.5 collective-permute-start.5
  25.0 1.0 %collective-permute-done.4.refs_2_ = bf16[16,7296]{1,0:T(8,128)(2,1)S(1)} collective-permute-done((bf16[16,7296]{1,0:T(8,128)(2,1)S(1)}, bf16[16,7296]{1,0:T(8,128)(2,1)S(1)}, u32[]{:S(2)}, u32[]{:S(2)}) %collective-permute-start.4) | collective-permute-done | bytes 233504 | tf_op jit(solution)/shard_map/ppermute | solution.py:19
  26.0 0.3 collective-permute-done.5.refs_3_
  26.4 10.9 %experts.1 = (bf16[16,7168]{1,0:T(8,128)(2,1)S(1)}, bf16[16,7168]{1,0:T(8,128)(2,1)S(1)}, bf16[32,7168]{1,0:T(8,128)(2,1)S(1)}) custom-call(bf16[16,7296]{1,0:T(8,128)(2,1)S(1)} %pad_maximum_fusion.refs_0_, bf16[16,7296]{1,0:T(8,128)(2,1)S(1)} %collective-permute-done.3.refs_1_, bf16[16,7296]{1,0:T(8,128)(2,1)S(1)} %collective-permute-done.4.refs_2_, ...), custom_call_target="tpu_custom_call" | custom-call | flops 2818572288 | bytes 44040192 | tf_op jit(solution)/shard_map/experts/pallas_call | solution.py:184
  37.2 0.2 collective-permute-start.6
  37.5 1.6 %collective-permute-done.6 = bf16[32,7168]{1,0:T(8,128)(2,1)S(1)} collective-permute-done((bf16[32,7168]{1,0:T(8,128)(2,1)S(1)}, bf16[32,7168]{1,0:T(8,128)(2,1)S(1)}, u32[]{:S(2)}, u32[]{:S(2)}) %collective-permute-start.6) | collective-permute-done | bytes 458784 | tf_op jit(solution)/shard_map/ppermute | solution.py:19
  39.1 0.1 add_convert_fusion.1
  39.2 1.1 %collective-permute-start.7 = (bf16[16,7168]{1,0:T(8,128)(2,1)S(1)}, bf16[16,7168]{1,0:T(8,128)(2,1)S(1)}, u32[]{:S(2)}, u32[]{:S(2)}) collective-permute-start(bf16[16,7168]{1,0:T(8,128)(2,1)S(1)} %add_convert_fusion.1), channel_id=1, source_target_pairs={{0,2},{1,3},{2,0},{3,1},{4,6},{5,7},{6,4},{7,5},{8,10},{9,11},{10,... | collective-permute-start | bytes 688136 | tf_op jit(solution)/shard_map/ppermute | solution.py:19
  40.2 6.7 %collective-permute-done.7 = bf16[16,7168]{1,0:T(8,128)(2,1)S(1)} collective-permute-done((bf16[16,7168]{1,0:T(8,128)(2,1)S(1)}, bf16[16,7168]{1,0:T(8,128)(2,1)S(1)}, u32[]{:S(2)}, u32[]{:S(2)}) %collective-permute-start.7) | collective-permute-done | bytes 229408 | tf_op jit(solution)/shard_map/ppermute | solution.py:19
  46.9 0.1 add_convert_fusion
  47.0 0.1 fusion
  47.1 1.3 %collective-permute-start.8 = (bf16[4,7168]{1,0:T(4,128)(2,1)S(1)}, bf16[4,7168]{1,0:T(4,128)(2,1)S(1)}, u32[]{:S(2)}, u32[]{:S(2)}) collective-permute-start(bf16[4,7168]{1,0:T(4,128)(2,1)S(1)} %get-tuple-element.30), channel_id=1, source_target_pairs={{0,4},{4,0},{8,12},{12,8},{1,5},{5,1},{9,13},{13,9},{2,6},{6,2},{1... | collective-permute-start | bytes 172040 | tf_op jit(solution)/shard_map/ppermute | solution.py:21
  48.4 2.4 %collective-permute-start.10 = (bf16[4,7168]{1,0:T(4,128)(2,1)S(1)}, bf16[4,7168]{1,0:T(4,128)(2,1)S(1)}, u32[]{:S(2)}, u32[]{:S(2)}) collective-permute-start(bf16[4,7168]{1,0:T(4,128)(2,1)S(1)} %get-tuple-element.31), channel_id=1, source_target_pairs={{0,12},{4,8},{8,4},{12,0},{1,13},{5,9},{9,5},{13,1},{2,14},{6,10},... | collective-permute-start | bytes 172040 | tf_op jit(solution)/shard_map/ppermute | solution.py:21
  50.8 0.5 collective-permute-start.9
  51.3 0.0 collective-permute-done.8
  51.3 3.6 %collective-permute-done.10 = bf16[4,7168]{1,0:T(4,128)(2,1)S(1)} collective-permute-done((bf16[4,7168]{1,0:T(4,128)(2,1)S(1)}, bf16[4,7168]{1,0:T(4,128)(2,1)S(1)}, u32[]{:S(2)}, u32[]{:S(2)}) %collective-permute-start.10) | collective-permute-done | bytes 57376 | tf_op jit(solution)/shard_map/ppermute | solution.py:21
  54.9 1.6 %collective-permute-done.9 = bf16[4,7168]{1,0:T(4,128)(2,1)S(1)} collective-permute-done((bf16[4,7168]{1,0:T(4,128)(2,1)S(1)}, bf16[4,7168]{1,0:T(4,128)(2,1)S(1)}, u32[]{:S(2)}, u32[]{:S(2)}) %collective-permute-start.9) | collective-permute-done | bytes 57376 | tf_op jit(solution)/shard_map/ppermute | solution.py:21
  56.5 0.7 %add_convert_fusion.3 = bf16[4,7168]{1,0:T(4,128)(2,1)} fusion(bf16[4,7168]{1,0:T(4,128)(2,1)S(1)} %collective-permute-done.10, bf16[4,7168]{1,0:T(4,128)(2,1)S(1)} %collective-permute-done.9, bf16[4,7168]{1,0:T(4,128)(2,1)S(1)} %collective-permute-done.8, bf16[16,7168]{1,0:T(8,128)(2,1)S(1)} %add_convert_fusion), kind=kLoop, calls=%fused_computation.4 | loop fusion | flops 229376 | bytes 286720 | tf_op jit(solution)/shard_map/convert_element_type | solution.py:208
Async XLA Ops:
  0.6 0.8 %copy-start = (bf16[4,7168]{1,0:T(4,128)(2,1)S(1)}, bf16[4,7168]{1,0:T(4,128)(2,1)}, u32[]{:S(2)}) copy-start(bf16[4,7168]{1,0:T(4,128)(2,1)} %tokens.1) | copy-start | bytes 172036
  1.4 0.7 %copy-start.1 = (s32[4,4]{1,0:T(4,128)S(1)}, s32[4,4]{1,0:T(4,128)}, u32[]{:S(2)}) copy-start(s32[4,4]{1,0:T(4,128)} %routes.1) | copy-start | bytes 196
  2.1 0.7 %copy-start.2 = (bf16[4,4]{1,0:T(4,128)(2,1)S(1)}, bf16[4,4]{1,0:T(4,128)(2,1)}, u32[]{:S(2)}) copy-start(bf16[4,4]{1,0:T(4,128)(2,1)} %gates.1) | copy-start | bytes 100
  2.9 14.4 %collective-permute-start.2 = (bf16[4,7296]{1,0:T(4,128)(2,1)S(1)}, bf16[4,7296]{1,0:T(4,128)(2,1)S(1)}, u32[]{:S(2)}, u32[]{:S(2)}) collective-permute-start(bf16[4,7296]{1,0:T(4,128)(2,1)S(1)} %pack.1), channel_id=1, source_target_pairs={{0,12},{4,8},{8,4},{12,0},{1,13},{5,9},{9,5},{13,1},{2,14},{6,10},... | collective-permute-start | bytes 175112 | tf_op jit(solution)/shard_map/ppermute | solution.py:21
  8.0 9.3 %collective-permute-start.1 = (bf16[4,7296]{1,0:T(4,128)(2,1)S(1)}, bf16[4,7296]{1,0:T(4,128)(2,1)S(1)}, u32[]{:S(2)}, u32[]{:S(2)}) collective-permute-start(bf16[4,7296]{1,0:T(4,128)(2,1)S(1)} %pack.1), channel_id=1, source_target_pairs={{0,8},{4,12},{8,0},{12,4},{1,9},{5,13},{9,1},{13,5},{2,10},{6,14},... | collective-permute-start | bytes 175112 | tf_op jit(solution)/shard_map/ppermute | solution.py:21
  8.0 9.3 %collective-permute-start = (bf16[4,7296]{1,0:T(4,128)(2,1)S(1)}, bf16[4,7296]{1,0:T(4,128)(2,1)S(1)}, u32[]{:S(2)}, u32[]{:S(2)}) collective-permute-start(bf16[4,7296]{1,0:T(4,128)(2,1)S(1)} %pack.1), channel_id=1, source_target_pairs={{0,4},{4,0},{8,12},{12,8},{1,5},{5,1},{9,13},{13,9},{2,6},{6,2},{1... | collective-permute-start | bytes 175112 | tf_op jit(solution)/shard_map/ppermute | solution.py:21
  8.7 0.7 %copy-start.3 = (s32[2]{0:T(128)S(1)}, s32[2]{0:T(128)}, u32[]{:S(2)}) copy-start(s32[2]{0:T(128)} %lengths.1) | copy-start | bytes 28
  17.4 7.1 %collective-permute-start.3 = (bf16[16,7296]{1,0:T(8,128)(2,1)S(1)}, bf16[16,7296]{1,0:T(8,128)(2,1)S(1)}, u32[]{:S(2)}, u32[]{:S(2)}) collective-permute-start(bf16[16,7296]{1,0:T(8,128)(2,1)S(1)} %pad_maximum_fusion.refs_0_), channel_id=1, source_target_pairs={{0,2},{1,3},{2,0},{3,1},{4,6},{5,7},{6,4},{7,5},{8,10},{9,11},{10,... | collective-permute-start | bytes 700424 | tf_op jit(solution)/shard_map/ppermute | solution.py:19
  24.5 1.6 %collective-permute-start.4 = (bf16[16,7296]{1,0:T(8,128)(2,1)S(1)}, bf16[16,7296]{1,0:T(8,128)(2,1)S(1)}, u32[]{:S(2)}, u32[]{:S(2)}) collective-permute-start(bf16[16,7296]{1,0:T(8,128)(2,1)S(1)} %pad_maximum_fusion.refs_0_), channel_id=1, source_target_pairs={{0,1},{1,0},{2,3},{3,2},{4,5},{5,4},{6,7},{7,6},{8,9},{9,8},{10,11... | collective-permute-start | bytes 700424 | tf_op jit(solution)/shard_map/ppermute | solution.py:19
  24.5 1.8 %collective-permute-start.5 = (bf16[16,7296]{1,0:T(8,128)(2,1)S(1)}, bf16[16,7296]{1,0:T(8,128)(2,1)S(1)}, u32[]{:S(2)}, u32[]{:S(2)}) collective-permute-start(bf16[16,7296]{1,0:T(8,128)(2,1)S(1)} %collective-permute-done.3.refs_1_), channel_id=1, source_target_pairs={{0,1},{1,0},{2,3},{3,2},{4,5},{5,4},{6,7},{7,6},{8,9},{9,8},{10,11... | collective-permute-start | bytes 700424 | tf_op jit(solution)/shard_map/ppermute | solution.py:19
  37.2 1.9 %collective-permute-start.6 = (bf16[32,7168]{1,0:T(8,128)(2,1)S(1)}, bf16[32,7168]{1,0:T(8,128)(2,1)S(1)}, u32[]{:S(2)}, u32[]{:S(2)}) collective-permute-start(bf16[32,7168]{1,0:T(8,128)(2,1)S(1)} %get-tuple-element.27), channel_id=1, source_target_pairs={{0,1},{1,0},{2,3},{3,2},{4,5},{5,4},{6,7},{7,6},{8,9},{9,8},{10,11... | collective-permute-start | bytes 1376264 | tf_op jit(solution)/shard_map/ppermute | solution.py:19
  39.2 7.8 %collective-permute-start.7 = (bf16[16,7168]{1,0:T(8,128)(2,1)S(1)}, bf16[16,7168]{1,0:T(8,128)(2,1)S(1)}, u32[]{:S(2)}, u32[]{:S(2)}) collective-permute-start(bf16[16,7168]{1,0:T(8,128)(2,1)S(1)} %add_convert_fusion.1), channel_id=1, source_target_pairs={{0,2},{1,3},{2,0},{3,1},{4,6},{5,7},{6,4},{7,5},{8,10},{9,11},{10,... | collective-permute-start | bytes 688136 | tf_op jit(solution)/shard_map/ppermute | solution.py:19
  47.1 4.2 %collective-permute-start.8 = (bf16[4,7168]{1,0:T(4,128)(2,1)S(1)}, bf16[4,7168]{1,0:T(4,128)(2,1)S(1)}, u32[]{:S(2)}, u32[]{:S(2)}) collective-permute-start(bf16[4,7168]{1,0:T(4,128)(2,1)S(1)} %get-tuple-element.30), channel_id=1, source_target_pairs={{0,4},{4,0},{8,12},{12,8},{1,5},{5,1},{9,13},{13,9},{2,6},{6,2},{1... | collective-permute-start | bytes 172040 | tf_op jit(solution)/shard_map/ppermute | solution.py:21
  48.4 6.5 %collective-permute-start.10 = (bf16[4,7168]{1,0:T(4,128)(2,1)S(1)}, bf16[4,7168]{1,0:T(4,128)(2,1)S(1)}, u32[]{:S(2)}, u32[]{:S(2)}) collective-permute-start(bf16[4,7168]{1,0:T(4,128)(2,1)S(1)} %get-tuple-element.31), channel_id=1, source_target_pairs={{0,12},{4,8},{8,4},{12,0},{1,13},{5,9},{9,5},{13,1},{2,14},{6,10},... | collective-permute-start | bytes 172040 | tf_op jit(solution)/shard_map/ppermute | solution.py:21
  50.8 5.7 %collective-permute-start.9 = (bf16[4,7168]{1,0:T(4,128)(2,1)S(1)}, bf16[4,7168]{1,0:T(4,128)(2,1)S(1)}, u32[]{:S(2)}, u32[]{:S(2)}) collective-permute-start(bf16[4,7168]{1,0:T(4,128)(2,1)S(1)} %get-tuple-element.32), channel_id=1, source_target_pairs={{0,8},{4,12},{8,0},{12,4},{1,9},{5,13},{9,1},{13,5},{2,10},{6,14},... | collective-permute-start | bytes 172040 | tf_op jit(solution)/shard_map/ppermute | solution.py:21

commit v2 on v1

v2 whole, which is shorter than its diff:
```python
import functools

import jax
import jax.numpy as jnp
from jax import lax
from jax.experimental import pallas as pl
from jax.experimental.pallas import tpu as pltpu
from jax.sharding import PartitionSpec as P

SCORE_SCALE = 192.0 ** (-0.5)
BF16 = jnp.bfloat16
F32 = jnp.float32
LANES = 128


def swap(x, side_bits, dev_bits):
    side, dev = lax.axis_size("side"), lax.axis_size("dev")
    if side_bits == 0:
        return lax.ppermute(x, "dev", [(i, i ^ dev_bits) for i in range(dev)])
    if dev_bits == 0:
        return lax.ppermute(x, "side", [(i, i ^ side_bits) for i in range(side)])
    pairs = [(i, i ^ (side_bits * dev + dev_bits)) for i in range(side * dev)]
    return lax.ppermute(x, ("side", "dev"), pairs)


def in_hbm(x):
    return pltpu.with_memory_space_constraint(x, pltpu.HBM)


def in_vmem(x):
    return pltpu.with_memory_space_constraint(x, pltpu.VMEM)


HBM = pl.BlockSpec(memory_space=pltpu.HBM)
VMEM = pl.BlockSpec(memory_space=pltpu.VMEM)
MIB = 1024 * 1024


def pack_kernel(tokens, routes, gates, out, tokens_here, routes_here, gates_here, sems):
    pairs = ((tokens, tokens_here), (routes, routes_here), (gates, gates_here))
    copies = [pltpu.make_async_copy(a, b, sems.at[i]) for i, (a, b) in enumerate(pairs)]
    for copy in copies:
        copy.start()
    for copy in copies:
        copy.wait()
    width = tokens.shape[1]
    out[:, :width] = tokens_here[...]
    lane = lax.broadcasted_iota(jnp.int32, (tokens.shape[0], out.shape[1] - width), 1)
    total = jnp.zeros(lane.shape, F32)
    gate = gates_here[...].astype(F32)
    for k in range(routes.shape[1]):
        total = total + jnp.where(routes_here[:, k : k + 1] == lane, gate[:, k : k + 1], 0.0)
    out[:, width:] = total.astype(BF16)


def pack(tokens, routes, gates, experts):
    rows, width = tokens.shape
    pad = -(-experts // LANES) * LANES
    arrays = (tokens, routes, gates)
    return pl.pallas_call(
        pack_kernel,
        out_shape=pltpu.VMEM((rows, width + pad), BF16),
        in_specs=[HBM] * 3,
        out_specs=VMEM,
        scratch_shapes=[pltpu.VMEM(x.shape, x.dtype) for x in arrays] + [pltpu.SemaphoreType.DMA((3,))],
        compiler_params=pltpu.CompilerParams(vmem_limit_bytes=2 * MIB),
        name="pack",
    )(*[in_hbm(x) for x in arrays])


def chunks_of(width):
    step = 1024 if width % 1024 == 0 else width
    return step, width // step


def fetch_copies(e, w_in, held, sems):
    step, count = chunks_of(w_in.shape[2])
    return [
        pltpu.make_async_copy(
            w_in.at[e, g, pl.ds(i * step, step)], held.at[g, pl.ds(i * step, step)], sems.at[g * count + i]
        )
        for i in range(count)
        for g in range(2)
    ]


def fetch_kernel(e, w_in, held, sems):
    copies = fetch_copies(e, w_in, held, sems)
    for copy in copies:
        copy.start()
    for copy in copies:
        copy.wait()


def fetch(e, w_in):
    _, _, width, block = w_in.shape
    return pl.pallas_call(
        functools.partial(fetch_kernel, e),
        out_shape=pltpu.VMEM((2, width, block), BF16),
        in_specs=[HBM],
        out_specs=VMEM,
        scratch_shapes=[pltpu.SemaphoreType.DMA((2 * chunks_of(width)[1],))],
        compiler_params=pltpu.CompilerParams(vmem_limit_bytes=2 * MIB),
        cost_estimate=pl.CostEstimate(flops=0, bytes_accessed=FETCH_COST * 4 * width * block, transcendentals=0),
        name="fetch",
    )(in_hbm(w_in))


FETCH_COST = 0


def attend_kernel(lengths, queries, rope_queries, latents, ropes, attended, q, qr, c, cr, out, sems, out_sems):
    pairs = ((queries, q), (rope_queries, qr), (latents, c), (ropes, cr))
    count = q.shape[0]
    copies = [
        [pltpu.make_async_copy(a.at[r], b.at[r], sems.at[r, i]) for i, (a, b) in enumerate(pairs)]
        for r in range(count)
    ]
    for request in copies:
        for copy in request:
            copy.start()
    results = []
    for r in range(count):
        for copy in copies[r]:
            copy.wait()
        latent = c[r]
        scores = lax.dot_general(
            q[r], latent, (((1,), (1,)), ((), ())), preferred_element_type=F32
        ) + lax.dot_general(qr[r], cr[r], (((0,), (0,)), ((), ())), preferred_element_type=F32)
        scores = scores * SCORE_SCALE
        place = lax.broadcasted_iota(jnp.int32, scores.shape, 1)
        scores = jnp.where(place < lengths[r], scores, -jnp.inf)
        shifted = jnp.exp(scores - jnp.max(scores, axis=1, keepdims=True))
        shares = (shifted / jnp.sum(shifted, axis=1, keepdims=True)).astype(BF16)
        out[r] = jnp.dot(shares, latent, preferred_element_type=F32).astype(BF16)
        results.append(pltpu.make_async_copy(out.at[r], attended.at[r], out_sems.at[r]))
        results[-1].start()
    for copy in results:
        copy.wait()


def attend(query_latent, query_rope, cache_latent, cache_rope, lengths):
    arrays = (query_latent, query_rope, cache_latent, cache_rope)
    count = query_latent.shape[0]
    return pl.pallas_call(
        attend_kernel,
        out_shape=pltpu.HBM(query_latent.shape, BF16),
        in_specs=[pl.BlockSpec(memory_space=pltpu.SMEM)] + [HBM] * 4,
        out_specs=HBM,
        scratch_shapes=[pltpu.VMEM(x.shape, BF16) for x in (*arrays, query_latent)]
        + [pltpu.SemaphoreType.DMA((count, 4)), pltpu.SemaphoreType.DMA((count,))],
        compiler_params=pltpu.CompilerParams(vmem_limit_bytes=8 * MIB),
        name="attend",
    )(in_hbm(lengths), *[in_hbm(x) for x in arrays])


def experts_kernel(pieces, count, *refs):
    parts, refs = refs[:pieces], refs[pieces:]
    w_in, held, outs = refs[:count], refs[count], refs[count + 1 : -2]
    rows, act = refs[-2:]
    _, block, width = held.shape
    step, chunks = chunks_of(width)
    size = parts[0].shape[0]
    for i, part in enumerate(parts):
        rows[i * size : (i + 1) * size, :] = part[...]
    first = lax.axis_index("side") * count
    gates = rows[:, width:].astype(F32)
    lane = lax.broadcasted_iota(jnp.int32, gates.shape, 1)
    for e in range(count):
        gate = jnp.dot(rows[:, :width], w_in[e][0], preferred_element_type=F32)
        up = jnp.dot(rows[:, :width], w_in[e][1], preferred_element_type=F32)
        weight = jnp.sum(jnp.where(lane == first + e, gates, 0.0), axis=1, keepdims=True)
        value = gate / (1.0 + jnp.exp(-gate)) * up * weight
        act[:, e * block : (e + 1) * block] = value.astype(BF16)
    for i in range(chunks):
        at = slice(i * step, (i + 1) * step)
        total = jnp.dot(act[:, :block], held[0, :, at], preferred_element_type=F32)
        for e in range(1, count):
            total = total + jnp.dot(
                act[:, e * block : (e + 1) * block], held[e, :, at], preferred_element_type=F32
            )
        total = total.astype(BF16)
        start = 0
        for out in outs:
            out[:, at] = total[start : start + out.shape[0]]
            start += out.shape[0]


def run_experts(near, far, w_in, w_out):
    parts = [*near, *far]
    size, packed = parts[0].shape
    total = size * len(parts)
    count, block, width = w_out.shape
    room = 2 * MIB + total * (2 * packed + 2 * count * block + 8 * chunks_of(width)[0])
    outs = [pltpu.VMEM((size, width), BF16) for _ in near] + [pltpu.VMEM((size * len(far), width), BF16)]
    results = pl.pallas_call(
        functools.partial(experts_kernel, len(parts), count),
        out_shape=outs,
        in_specs=[VMEM] * (len(parts) + count + 1),
        out_specs=[VMEM] * len(outs),
        scratch_shapes=[
            pltpu.VMEM((total, packed), BF16),
            pltpu.VMEM((total, count * block), BF16),
        ],
        compiler_params=pltpu.CompilerParams(vmem_limit_bytes=room),
        cost_estimate=pl.CostEstimate(
            flops=6 * total * count * width * block, bytes_accessed=6 * count * width * block, transcendentals=0
        ),
        name="experts",
    )(*[in_vmem(x) for x in parts], *[in_vmem(w) for w in w_in], w_out)
    return results[:-1], results[-1]


def add(*terms):
    total = terms[0].astype(F32)
    for term in terms[1:]:
        total = total + term.astype(F32)
    return total.astype(BF16)


def shards(
    tokens,
    routes,
    gate_weights,
    experts_in,
    experts_out,
    query_latent,
    query_rope,
    cache_latent,
    cache_rope,
    lengths,
):
    side, dev = lax.axis_size("side"), lax.axis_size("dev")
    chips = dev // 2
    count = tokens.shape[0]
    packed = pack(tokens, routes, gate_weights, experts_in.shape[0] * side)
    along = [packed] + [swap(packed, k, 0) for k in range(1, side)]
    first = fetch(0, experts_in)
    *along, first = lax.optimization_barrier((*along, first))
    along = jnp.concatenate(along)
    near = [along] + [swap(along, 0, 2 * k) for k in range(1, chips)]
    others = [fetch(e, experts_in) for e in range(1, experts_in.shape[0])]
    far = [swap(near[0], 0, 1)]
    near, others = lax.optimization_barrier((near, others))
    far += [swap(piece, 0, 1) for piece in near[1:]]
    weights = [first] + others
    near_part, far_part = run_experts(near, far, weights, experts_out)
    far_part = swap(far_part, 0, 1)
    size = side * count
    both = [add(part, far_part[k * size : (k + 1) * size]) for k, part in enumerate(near_part)]
    across = [swap(both[k], 0, 2 * k) for k in range(1, chips)]
    attended = attend(query_latent, query_rope, cache_latent, cache_rope, lengths)
    across, attended = lax.optimization_barrier((across, attended))
    column = add(both[0], *across)
    routed_out = add(
        column[:count],
        *[swap(column[k * count : (k + 1) * count], k, 0) for k in range(1, side)],
    )
    return (routed_out, attended)


def solution(mesh):
    return jax.shard_map(
        shards,
        mesh=mesh,
        in_specs=(
            P(("groups", "side", "dev"), None),
            P(("groups", "side", "dev"), None),
            P(("groups", "side", "dev"), None),
            P("side", None, None, "dev"),
            P("side", "dev", None),
            P(("groups", "side", "dev"), None, None),
            P(("groups", "side", "dev"), None, None),
            P(("groups", "side", "dev"), None, None),
            P(("groups", "side", "dev"), None, None),
            P(("groups", "side", "dev")),
        ),
        out_specs=(P(("groups", "side", "dev"), None), P(("groups", "side", "dev"), None, None)),
        check_vma=False,
    )
```

time: 57.4 us -> 49.9 us (0.87)
  waiting for transfers between devices: 14.9 us -> 9.88 us
  local copies, waits for them, and re-layouts: 2.9 us -> 0.09 us
    ppermute x5, waiting for transfers between devices: 9.63 us -> 5.33 us  [swap(): return lax.ppermute(x, 'dev', [(i, i ^ dev_bits) for i in range(dev)])]
    pallas_call x1, Pallas kernels: 10.9 us -> 7.8 us  [run_experts(): pl.pallas_call(functools.partial(experts_kernel, len(parts), count), out_...]
    pallas_call x3 -> x4, Pallas kernels: 13.3 us -> 16.3 us  [the longest x2 11.4 us: fetch(): pl.pallas_call(functools.partial(fetch_kernel, e), out_shape=pltpu.VMEM((...]
    unnamed x8, local copies, waits for them, and re-layouts: 2.83 us -> 0.02 us
    ppermute x6, waiting for transfers between devices: 5.23 us -> 4.55 us  [swap(): return lax.ppermute(x, 'side', [(i, i ^ side_bits) for i in range(side)])]
  transfers between devices with their start and end apart: 11 -> 11, of which waited for: 6 -> 8; matrix products, arithmetic and copies ran while one was open for 0% -> 0% of each run, Pallas kernels for 23% -> 31%
where the time goes in v2:
time: 49.9 us; the launch traced here: 49.7 us
  Pallas kernels  24.1 us (48%)
  starting transfers between devices  13.9 us (28%)
  waiting for transfers between devices  9.88 us (20%)
  other arithmetic  0.97 us (2%)
  between operations  0.77 us (2%)
    pallas_call x2, Pallas kernels, fetch(): pl.pallas_call(functools.partial(fetch_kernel, e), out_shape=pltpu.VMEM((...  11.4 us
    ppermute x6, starting transfers between devices, swap(): return lax.ppermute(x, 'side', [(i, i ^ side_bits) for i in range(side)])  10.1 us
    pallas_call x1, Pallas kernels, run_experts(): pl.pallas_call(functools.partial(experts_kernel, len(parts), count), out_...  7.8 us
    ppermute x5, waiting for transfers between devices, swap(): return lax.ppermute(x, 'dev', [(i, i ^ dev_bits) for i in range(dev)])  5.33 us
    ppermute x6, waiting for transfers between devices, swap(): return lax.ppermute(x, 'side', [(i, i ^ side_bits) for i in range(side)])  4.55 us
    pallas_call x1, Pallas kernels, attend(): pl.pallas_call(attend_kernel, out_shape=pltpu.HBM(query_latent.shape, BF1...  4 us
    ppermute x5, starting transfers between devices, swap(): return lax.ppermute(x, 'dev', [(i, i ^ dev_bits) for i in range(dev)])  3.73 us
  transfers between devices with their start and end apart: 11, of which 8 were waited for; matrix products, arithmetic and copies ran while one was open for 0% of the time, Pallas kernels for 31%

profile of v2, /device:TPU:0, one launch (start us, length us, event | category | flops | bytes accessed | tf_op | source)
XLA Modules:
  0.0 49.7 jit_solution(3193382619695485182)
XLA Ops:
  0.6 0.9 %pack.1 = bf16[4,7296]{1,0:T(4,128)(2,1)S(1)} custom-call(bf16[4,7168]{1,0:T(4,128)(2,1)} %tokens.1, s32[4,4]{1,0:T(4,128)} %routes.1, bf16[4,4]{1,0:T(4,128)(2,1)} %gates.1), custom_call_target="tpu_custom_call" | custom-call | tf_op jit(solution)/shard_map/pack/pallas_call | solution.py:60
  1.6 3.1 %collective-permute-start = (bf16[4,7296]{1,0:T(4,128)(2,1)S(1)}, bf16[4,7296]{1,0:T(4,128)(2,1)S(1)}, u32[]{:S(2)}, u32[]{:S(2)}) collective-permute-start(bf16[4,7296]{1,0:T(4,128)(2,1)S(1)} %pack.1), channel_id=1, source_target_pairs={{0,4},{4,0},{8,12},{12,8},{1,5},{5,1},{9,13},{13,9},{2,6},{6,2},{1... | collective-permute-start | bytes 175112 | tf_op jit(solution)/shard_map/ppermute | solution.py:21
  4.7 2.6 %collective-permute-start.1 = (bf16[4,7296]{1,0:T(4,128)(2,1)S(1)}, bf16[4,7296]{1,0:T(4,128)(2,1)S(1)}, u32[]{:S(2)}, u32[]{:S(2)}) collective-permute-start(bf16[4,7296]{1,0:T(4,128)(2,1)S(1)} %pack.1), channel_id=1, source_target_pairs={{0,8},{4,12},{8,0},{12,4},{1,9},{5,13},{9,1},{13,5},{2,10},{6,14},... | collective-permute-start | bytes 175112 | tf_op jit(solution)/shard_map/ppermute | solution.py:21
  7.2 0.0 collective-permute-start.2
  7.3 5.3 %fetch.2.refs_4_ = bf16[2,7168,512]{2,1,0:T(8,128)(2,1)S(1)} custom-call(bf16[2,2,7168,512]{3,2,1,0:T(8,128)(2,1)} %w_in.3), custom_call_target="tpu_custom_call" | custom-call | tf_op jit(solution)/shard_map/fetch/pallas_call | solution.py:97
  12.6 0.0 collective-permute-done
  12.6 0.0 collective-permute-done.1
  12.6 0.6 %collective-permute-done.2 = bf16[4,7296]{1,0:T(4,128)(2,1)S(1)} collective-permute-done((bf16[4,7296]{1,0:T(4,128)(2,1)S(1)}, bf16[4,7296]{1,0:T(4,128)(2,1)S(1)}, u32[]{:S(2)}, u32[]{:S(2)}) %collective-permute-start.2) | collective-permute-done | bytes 58400 | tf_op jit(solution)/shard_map/ppermute | solution.py:21
  13.2 0.0 slice-start
  13.2 0.1 pad_maximum_fusion.refs_0_
  13.4 0.0 slice-start.1
  13.4 0.0 slice-start.2
  13.4 0.0 slice-start.3
  13.4 1.6 %collective-permute-start.3 = (bf16[16,7296]{1,0:T(8,128)(2,1)S(1)}, bf16[16,7296]{1,0:T(8,128)(2,1)S(1)}, u32[]{:S(2)}, u32[]{:S(2)}) collective-permute-start(bf16[16,7296]{1,0:T(8,128)(2,1)S(1)} %pad_maximum_fusion.refs_0_), channel_id=1, source_target_pairs={{0,2},{1,3},{2,0},{3,1},{4,6},{5,7},{6,4},{7,5},{8,10},{9,11},{10,... | collective-permute-start | bytes 700424 | tf_op jit(solution)/shard_map/ppermute | solution.py:19
  15.0 6.1 %fetch.3.refs_5_ = bf16[2,7168,512]{2,1,0:T(8,128)(2,1)S(1)} custom-call(bf16[2,2,7168,512]{3,2,1,0:T(8,128)(2,1)} %w_in.3), custom_call_target="tpu_custom_call" | custom-call | tf_op jit(solution)/shard_map/fetch/pallas_call | solution.py:97
  21.1 0.1 collective-permute-start.4
  21.1 0.0 collective-permute-done.3.refs_1_
  21.1 0.5 collective-permute-start.5
  21.6 1.0 %collective-permute-done.4.refs_2_ = bf16[16,7296]{1,0:T(8,128)(2,1)S(1)} collective-permute-done((bf16[16,7296]{1,0:T(8,128)(2,1)S(1)}, bf16[16,7296]{1,0:T(8,128)(2,1)S(1)}, u32[]{:S(2)}, u32[]{:S(2)}) %collective-permute-start.4) | collective-permute-done | bytes 233504 | tf_op jit(solution)/shard_map/ppermute | solution.py:19
  22.6 0.3 collective-permute-done.5.refs_3_
  23.0 0.0 slice-done
  23.0 0.0 slice-done.1
  23.0 0.0 slice-done.2
  23.0 0.0 slice-done.3
  23.0 7.8 %experts.1 = (bf16[16,7168]{1,0:T(8,128)(2,1)S(1)}, bf16[16,7168]{1,0:T(8,128)(2,1)S(1)}, bf16[32,7168]{1,0:T(8,128)(2,1)S(1)}) custom-call(bf16[16,7296]{1,0:T(8,128)(2,1)S(1)} %pad_maximum_fusion.refs_0_, bf16[16,7296]{1,0:T(8,128)(2,1)S(1)} %collective-permute-done.3.refs_1_, bf16[16,7296]{1,0:T(8,128)(2,1)S(1)} %collective-permute-done.4.refs_2_, ...), custom_call_target="tpu_custom_call" | custom-call | flops 2818572288 | bytes 44040192 | tf_op jit(solution)/shard_map/experts/pallas_call | solution.py:196
  30.8 0.2 collective-permute-start.6
  31.0 1.6 %collective-permute-done.6 = bf16[32,7168]{1,0:T(8,128)(2,1)S(1)} collective-permute-done((bf16[32,7168]{1,0:T(8,128)(2,1)S(1)}, bf16[32,7168]{1,0:T(8,128)(2,1)S(1)}, u32[]{:S(2)}, u32[]{:S(2)}) %collective-permute-start.6) | collective-permute-done | bytes 458784 | tf_op jit(solution)/shard_map/ppermute | solution.py:19
  32.7 0.1 add_convert_fusion.1
  32.7 1.4 %collective-permute-start.7 = (bf16[16,7168]{1,0:T(8,128)(2,1)S(1)}, bf16[16,7168]{1,0:T(8,128)(2,1)S(1)}, u32[]{:S(2)}, u32[]{:S(2)}) collective-permute-start(bf16[16,7168]{1,0:T(8,128)(2,1)S(1)} %add_convert_fusion.1), channel_id=1, source_target_pairs={{0,2},{1,3},{2,0},{3,1},{4,6},{5,7},{6,4},{7,5},{8,10},{9,11},{10,... | collective-permute-start | bytes 688136 | tf_op jit(solution)/shard_map/ppermute | solution.py:19
  34.1 4.0 %attend.1 = bf16[2,128,512]{2,1,0:T(8,128)(2,1)} custom-call(s32[2]{0:T(128)} %lengths.1, bf16[2,128,512]{2,1,0:T(8,128)(2,1)} %queries.1, bf16[2,64,128]{2,1,0:T(8,128)(2,1)} %rope_queries.1, bf16[2,512,512]{2,1,0:T(8,128)(2,1)} %latents.1, bf16[2,64,512]{2,1,0:T(8,128)(2,1)} %ropes.1), custom_call_target="tpu_custom_call" | custom-call | tf_op jit(solution)/shard_map/attend/pallas_call | solution.py:145
  38.1 2.4 %collective-permute-done.7 = bf16[16,7168]{1,0:T(8,128)(2,1)S(1)} collective-permute-done((bf16[16,7168]{1,0:T(8,128)(2,1)S(1)}, bf16[16,7168]{1,0:T(8,128)(2,1)S(1)}, u32[]{:S(2)}, u32[]{:S(2)}) %collective-permute-start.7) | collective-permute-done | bytes 229408 | tf_op jit(solution)/shard_map/ppermute | solution.py:19
  40.5 0.1 add_convert_fusion
  40.6 0.1 fusion
  40.7 3.3 %collective-permute-start.10 = (bf16[4,7168]{1,0:T(4,128)(2,1)S(1)}, bf16[4,7168]{1,0:T(4,128)(2,1)S(1)}, u32[]{:S(2)}, u32[]{:S(2)}) collective-permute-start(bf16[4,7168]{1,0:T(4,128)(2,1)S(1)} %get-tuple-element.29), channel_id=1, source_target_pairs={{0,12},{4,8},{8,4},{12,0},{1,13},{5,9},{9,5},{13,1},{2,14},{6,10},... | collective-permute-start | bytes 172040 | tf_op jit(solution)/shard_map/ppermute | solution.py:21
  43.9 0.0 collective-permute-start.8
  43.9 1.2 %collective-permute-start.9 = (bf16[4,7168]{1,0:T(4,128)(2,1)S(1)}, bf16[4,7168]{1,0:T(4,128)(2,1)S(1)}, u32[]{:S(2)}, u32[]{:S(2)}) collective-permute-start(bf16[4,7168]{1,0:T(4,128)(2,1)S(1)} %get-tuple-element.30), channel_id=1, source_target_pairs={{0,8},{4,12},{8,0},{12,4},{1,9},{5,13},{9,1},{13,5},{2,10},{6,14},... | collective-permute-start | bytes 172040 | tf_op jit(solution)/shard_map/ppermute | solution.py:21
  45.1 1.7 %collective-permute-done.10 = bf16[4,7168]{1,0:T(4,128)(2,1)S(1)} collective-permute-done((bf16[4,7168]{1,0:T(4,128)(2,1)S(1)}, bf16[4,7168]{1,0:T(4,128)(2,1)S(1)}, u32[]{:S(2)}, u32[]{:S(2)}) %collective-permute-start.10) | collective-permute-done | bytes 57376 | tf_op jit(solution)/shard_map/ppermute | solution.py:21
  46.8 1.3 %collective-permute-done.8 = bf16[4,7168]{1,0:T(4,128)(2,1)S(1)} collective-permute-done((bf16[4,7168]{1,0:T(4,128)(2,1)S(1)}, bf16[4,7168]{1,0:T(4,128)(2,1)S(1)}, u32[]{:S(2)}, u32[]{:S(2)}) %collective-permute-start.8) | collective-permute-done | bytes 57376 | tf_op jit(solution)/shard_map/ppermute | solution.py:21
  48.1 0.9 %collective-permute-done.9 = bf16[4,7168]{1,0:T(4,128)(2,1)S(1)} collective-permute-done((bf16[4,7168]{1,0:T(4,128)(2,1)S(1)}, bf16[4,7168]{1,0:T(4,128)(2,1)S(1)}, u32[]{:S(2)}, u32[]{:S(2)}) %collective-permute-start.9) | collective-permute-done | bytes 57376 | tf_op jit(solution)/shard_map/ppermute | solution.py:21
  49.0 0.7 %add_convert_fusion.3 = bf16[4,7168]{1,0:T(4,128)(2,1)} fusion(bf16[4,7168]{1,0:T(4,128)(2,1)S(1)} %collective-permute-done.10, bf16[4,7168]{1,0:T(4,128)(2,1)S(1)} %collective-permute-done.9, bf16[4,7168]{1,0:T(4,128)(2,1)S(1)} %collective-permute-done.8, bf16[16,7168]{1,0:T(8,128)(2,1)S(1)} %add_convert_fusion), kind=kLoop, calls=%fused_computation.4 | loop fusion | flops 229376 | bytes 286720 | tf_op jit(solution)/shard_map/convert_element_type | solution.py:218
  (1 shorter events, 0.0 us)
Async XLA Ops:
  1.6 11.0 %collective-permute-start = (bf16[4,7296]{1,0:T(4,128)(2,1)S(1)}, bf16[4,7296]{1,0:T(4,128)(2,1)S(1)}, u32[]{:S(2)}, u32[]{:S(2)}) collective-permute-start(bf16[4,7296]{1,0:T(4,128)(2,1)S(1)} %pack.1), channel_id=1, source_target_pairs={{0,4},{4,0},{8,12},{12,8},{1,5},{5,1},{9,13},{13,9},{2,6},{6,2},{1... | collective-permute-start | bytes 175112 | tf_op jit(solution)/shard_map/ppermute | solution.py:21
  4.7 7.9 %collective-permute-start.1 = (bf16[4,7296]{1,0:T(4,128)(2,1)S(1)}, bf16[4,7296]{1,0:T(4,128)(2,1)S(1)}, u32[]{:S(2)}, u32[]{:S(2)}) collective-permute-start(bf16[4,7296]{1,0:T(4,128)(2,1)S(1)} %pack.1), channel_id=1, source_target_pairs={{0,8},{4,12},{8,0},{12,4},{1,9},{5,13},{9,1},{13,5},{2,10},{6,14},... | collective-permute-start | bytes 175112 | tf_op jit(solution)/shard_map/ppermute | solution.py:21
  7.2 6.0 %collective-permute-start.2 = (bf16[4,7296]{1,0:T(4,128)(2,1)S(1)}, bf16[4,7296]{1,0:T(4,128)(2,1)S(1)}, u32[]{:S(2)}, u32[]{:S(2)}) collective-permute-start(bf16[4,7296]{1,0:T(4,128)(2,1)S(1)} %pack.1), channel_id=1, source_target_pairs={{0,12},{4,8},{8,4},{12,0},{1,13},{5,9},{9,5},{13,1},{2,14},{6,10},... | collective-permute-start | bytes 175112 | tf_op jit(solution)/shard_map/ppermute | solution.py:21
  13.2 9.7 %slice-start = ((s8[14680064]{0:T(1024)(128)(4,1)}), s8[4194304]{0:T(1024)(128)(4,1)S(1)}, s32[]{:S(2)}) async-start(s8[14680064]{0:T(1024)(128)(4,1)} %bitcast), calls=%async_computation | async-start | bytes 8388608
  13.4 9.6 %slice-start.1 = ((s8[14680064]{0:T(1024)(128)(4,1)}), s8[4194304]{0:T(1024)(128)(4,1)S(1)}, s32[]{:S(2)}) async-start(s8[14680064]{0:T(1024)(128)(4,1)} %bitcast), calls=%async_computation.1 | async-start | bytes 8388608
  13.4 9.6 %slice-start.2 = ((s8[14680064]{0:T(1024)(128)(4,1)}), s8[4194304]{0:T(1024)(128)(4,1)S(1)}, s32[]{:S(2)}) async-start(s8[14680064]{0:T(1024)(128)(4,1)} %bitcast), calls=%async_computation.2 | async-start | bytes 8388608
  13.4 9.6 %slice-start.3 = ((s8[14680064]{0:T(1024)(128)(4,1)}), s8[2097152]{0:T(1024)(128)(4,1)S(1)}, s32[]{:S(2)}) async-start(s8[14680064]{0:T(1024)(128)(4,1)} %bitcast), calls=%async_computation.3 | async-start | bytes 4194304
  13.4 7.7 %collective-permute-start.3 = (bf16[16,7296]{1,0:T(8,128)(2,1)S(1)}, bf16[16,7296]{1,0:T(8,128)(2,1)S(1)}, u32[]{:S(2)}, u32[]{:S(2)}) collective-permute-start(bf16[16,7296]{1,0:T(8,128)(2,1)S(1)} %pad_maximum_fusion.refs_0_), channel_id=1, source_target_pairs={{0,2},{1,3},{2,0},{3,1},{4,6},{5,7},{6,4},{7,5},{8,10},{9,11},{10,... | collective-permute-start | bytes 700424 | tf_op jit(solution)/shard_map/ppermute | solution.py:19
  21.1 1.6 %collective-permute-start.4 = (bf16[16,7296]{1,0:T(8,128)(2,1)S(1)}, bf16[16,7296]{1,0:T(8,128)(2,1)S(1)}, u32[]{:S(2)}, u32[]{:S(2)}) collective-permute-start(bf16[16,7296]{1,0:T(8,128)(2,1)S(1)} %pad_maximum_fusion.refs_0_), channel_id=1, source_target_pairs={{0,1},{1,0},{2,3},{3,2},{4,5},{5,4},{6,7},{7,6},{8,9},{9,8},{10,11... | collective-permute-start | bytes 700424 | tf_op jit(solution)/shard_map/ppermute | solution.py:19
  21.1 1.8 %collective-permute-start.5 = (bf16[16,7296]{1,0:T(8,128)(2,1)S(1)}, bf16[16,7296]{1,0:T(8,128)(2,1)S(1)}, u32[]{:S(2)}, u32[]{:S(2)}) collective-permute-start(bf16[16,7296]{1,0:T(8,128)(2,1)S(1)} %collective-permute-done.3.refs_1_), channel_id=1, source_target_pairs={{0,1},{1,0},{2,3},{3,2},{4,5},{5,4},{6,7},{7,6},{8,9},{9,8},{10,11... | collective-permute-start | bytes 700424 | tf_op jit(solution)/shard_map/ppermute | solution.py:19
  30.8 1.9 %collective-permute-start.6 = (bf16[32,7168]{1,0:T(8,128)(2,1)S(1)}, bf16[32,7168]{1,0:T(8,128)(2,1)S(1)}, u32[]{:S(2)}, u32[]{:S(2)}) collective-permute-start(bf16[32,7168]{1,0:T(8,128)(2,1)S(1)} %get-tuple-element.24), channel_id=1, source_target_pairs={{0,1},{1,0},{2,3},{3,2},{4,5},{5,4},{6,7},{7,6},{8,9},{9,8},{10,11... | collective-permute-start | bytes 1376264 | tf_op jit(solution)/shard_map/ppermute | solution.py:19
  32.7 7.8 %collective-permute-start.7 = (bf16[16,7168]{1,0:T(8,128)(2,1)S(1)}, bf16[16,7168]{1,0:T(8,128)(2,1)S(1)}, u32[]{:S(2)}, u32[]{:S(2)}) collective-permute-start(bf16[16,7168]{1,0:T(8,128)(2,1)S(1)} %add_convert_fusion.1), channel_id=1, source_target_pairs={{0,2},{1,3},{2,0},{3,1},{4,6},{5,7},{6,4},{7,5},{8,10},{9,11},{10,... | collective-permute-start | bytes 688136 | tf_op jit(solution)/shard_map/ppermute | solution.py:19
  40.7 6.2 %collective-permute-start.10 = (bf16[4,7168]{1,0:T(4,128)(2,1)S(1)}, bf16[4,7168]{1,0:T(4,128)(2,1)S(1)}, u32[]{:S(2)}, u32[]{:S(2)}) collective-permute-start(bf16[4,7168]{1,0:T(4,128)(2,1)S(1)} %get-tuple-element.29), channel_id=1, source_target_pairs={{0,12},{4,8},{8,4},{12,0},{1,13},{5,9},{9,5},{13,1},{2,14},{6,10},... | collective-permute-start | bytes 172040 | tf_op jit(solution)/shard_map/ppermute | solution.py:21
  43.9 4.2 %collective-permute-start.8 = (bf16[4,7168]{1,0:T(4,128)(2,1)S(1)}, bf16[4,7168]{1,0:T(4,128)(2,1)S(1)}, u32[]{:S(2)}, u32[]{:S(2)}) collective-permute-start(bf16[4,7168]{1,0:T(4,128)(2,1)S(1)} %get-tuple-element.28), channel_id=1, source_target_pairs={{0,4},{4,0},{8,12},{12,8},{1,5},{5,1},{9,13},{13,9},{2,6},{6,2},{1... | collective-permute-start | bytes 172040 | tf_op jit(solution)/shard_map/ppermute | solution.py:21
  43.9 5.1 %collective-permute-start.9 = (bf16[4,7168]{1,0:T(4,128)(2,1)S(1)}, bf16[4,7168]{1,0:T(4,128)(2,1)S(1)}, u32[]{:S(2)}, u32[]{:S(2)}) collective-permute-start(bf16[4,7168]{1,0:T(4,128)(2,1)S(1)} %get-tuple-element.30), channel_id=1, source_target_pairs={{0,8},{4,12},{8,0},{12,4},{1,9},{5,13},{9,1},{13,5},{2,10},{6,14},... | collective-permute-start | bytes 172040 | tf_op jit(solution)/shard_map/ppermute | solution.py:21

commit v3 on v2

--- a/solution.py
+++ b/solution.py
@@ -73,40 +73,34 @@
     return step, width // step
 
 
-def fetch_copies(e, w_in, held, sems):
-    step, count = chunks_of(w_in.shape[2])
-    return [
+def fetch_kernel(e, first, w_in, *refs):
+    held, sems = refs[-2:]
+    step, _ = chunks_of(w_in.shape[2])
+    copies = [
         pltpu.make_async_copy(
-            w_in.at[e, g, pl.ds(i * step, step)], held.at[g, pl.ds(i * step, step)], sems.at[g * count + i]
+            w_in.at[e, g, pl.ds((first + i) * step, step)], held.at[g, pl.ds(i * step, step)], sems.at[g, i]
         )
-        for i in range(count)
+        for i in range(held.shape[1] // step)
         for g in range(2)
     ]
-
-
-def fetch_kernel(e, w_in, held, sems):
-    copies = fetch_copies(e, w_in, held, sems)
     for copy in copies:
         copy.start()
     for copy in copies:
         copy.wait()
 
 
-def fetch(e, w_in):
+def fetch(w_in, e, first, count, *ready):
     _, _, width, block = w_in.shape
+    step, _ = chunks_of(width)
     return pl.pallas_call(
-        functools.partial(fetch_kernel, e),
-        out_shape=pltpu.VMEM((2, width, block), BF16),
-        in_specs=[HBM],
+        functools.partial(fetch_kernel, e, first),
+        out_shape=pltpu.VMEM((2, count * step, block), BF16),
+        in_specs=[HBM] + [VMEM] * len(ready),
         out_specs=VMEM,
-        scratch_shapes=[pltpu.SemaphoreType.DMA((2 * chunks_of(width)[1],))],
+        scratch_shapes=[pltpu.SemaphoreType.DMA((2, count))],
         compiler_params=pltpu.CompilerParams(vmem_limit_bytes=2 * MIB),
-        cost_estimate=pl.CostEstimate(flops=0, bytes_accessed=FETCH_COST * 4 * width * block, transcendentals=0),
         name="fetch",
-    )(in_hbm(w_in))
-
-
-FETCH_COST = 0
+    )(in_hbm(w_in), *ready)
 
 
 def attend_kernel(lengths, queries, rope_queries, latents, ropes, attended, q, qr, c, cr, out, sems, out_sems):
@@ -154,11 +148,26 @@
     )(in_hbm(lengths), *[in_hbm(x) for x in arrays])
 
 
-def experts_kernel(pieces, count, *refs):
+def project(rows, parts, g):
+    total, start = None, 0
+    for part in parts:
+        size = part.shape[1]
+        term = jnp.dot(rows[:, start : start + size], part[g], preferred_element_type=F32)
+        total = term if total is None else total + term
+        start += size
+    return total
+
+
+def experts_kernel(pieces, held_parts, *refs):
     parts, refs = refs[:pieces], refs[pieces:]
-    w_in, held, outs = refs[:count], refs[count], refs[count + 1 : -2]
+    count = sum(held_parts)
+    flat, held, outs = refs[:count], refs[count], refs[count + 1 : -2]
     rows, act = refs[-2:]
-    _, block, width = held.shape
+    w_in, start = [], 0
+    for number in held_parts:
+        w_in.append(flat[start : start + number])
+        start += number
+    count, block, width = held.shape
     step, chunks = chunks_of(width)
     size = parts[0].shape[0]
     for i, part in enumerate(parts):
@@ -167,8 +176,7 @@
     gates = rows[:, width:].astype(F32)
     lane = lax.broadcasted_iota(jnp.int32, gates.shape, 1)
     for e in range(count):
-        gate = jnp.dot(rows[:, :width], w_in[e][0], preferred_element_type=F32)
-        up = jnp.dot(rows[:, :width], w_in[e][1], preferred_element_type=F32)
+        gate, up = [project(rows, w_in[e], g) for g in range(2)]
         weight = jnp.sum(jnp.where(lane == first + e, gates, 0.0), axis=1, keepdims=True)
         value = gate / (1.0 + jnp.exp(-gate)) * up * weight
         act[:, e * block : (e + 1) * block] = value.astype(BF16)
@@ -192,11 +200,11 @@
     total = size * len(parts)
     count, block, width = w_out.shape
     room = 2 * MIB + total * (2 * packed + 2 * count * block + 8 * chunks_of(width)[0])
-    outs = [pltpu.VMEM((size, width), BF16) for _ in near] + [pltpu.VMEM((size * len(far), width), BF16)]
+    outs = [pltpu.VMEM((size, width), BF16) for _ in parts]
     results = pl.pallas_call(
-        functools.partial(experts_kernel, len(parts), count),
+        functools.partial(experts_kernel, len(parts), tuple(len(x) for x in w_in)),
         out_shape=outs,
-        in_specs=[VMEM] * (len(parts) + count + 1),
+        in_specs=[VMEM] * (len(parts) + sum(len(x) for x in w_in) + 1),
         out_specs=[VMEM] * len(outs),
         scratch_shapes=[
             pltpu.VMEM((total, packed), BF16),
@@ -207,8 +215,8 @@
             flops=6 * total * count * width * block, bytes_accessed=6 * count * width * block, transcendentals=0
         ),
         name="experts",
-    )(*[in_vmem(x) for x in parts], *[in_vmem(w) for w in w_in], w_out)
-    return results[:-1], results[-1]
+    )(*[in_vmem(x) for x in parts], *[in_vmem(w) for x in w_in for w in x], w_out)
+    return results[: len(near)], results[len(near) :]
 
 
 def add(*terms):
@@ -234,24 +242,29 @@
     chips = dev // 2
     count = tokens.shape[0]
     packed = pack(tokens, routes, gate_weights, experts_in.shape[0] * side)
+    chunks = chunks_of(tokens.shape[1])[1]
+    last = 1 if chunks > 2 else 0
     along = [packed] + [swap(packed, k, 0) for k in range(1, side)]
-    first = fetch(0, experts_in)
+    first = fetch(experts_in, 0, 0, chunks - last)
     *along, first = lax.optimization_barrier((*along, first))
     along = jnp.concatenate(along)
     near = [along] + [swap(along, 0, 2 * k) for k in range(1, chips)]
-    others = [fetch(e, experts_in) for e in range(1, experts_in.shape[0])]
+    others = [fetch(experts_in, e, 0, chunks, experts_out) for e in range(1, experts_in.shape[0])]
     far = [swap(near[0], 0, 1)]
     near, others = lax.optimization_barrier((near, others))
     far += [swap(piece, 0, 1) for piece in near[1:]]
-    weights = [first] + others
+    weights = [[first]] + [[x] for x in others]
+    if last:
+        near, rest = lax.optimization_barrier((near, experts_in))
+        weights[0].append(fetch(rest, 0, chunks - last, last))
     near_part, far_part = run_experts(near, far, weights, experts_out)
-    far_part = swap(far_part, 0, 1)
-    size = side * count
-    both = [add(part, far_part[k * size : (k + 1) * size]) for k, part in enumerate(near_part)]
-    across = [swap(both[k], 0, 2 * k) for k in range(1, chips)]
+    both = [add(near_part[k], swap(far_part[k], 0, 1)) for k in range(1, chips)]
+    own_far, both = lax.optimization_barrier((far_part[0], both))
+    across = [swap(both[k - 1], 0, 2 * k) for k in range(1, chips)]
+    own = add(near_part[0], swap(own_far, 0, 1))
     attended = attend(query_latent, query_rope, cache_latent, cache_rope, lengths)
     across, attended = lax.optimization_barrier((across, attended))
-    column = add(both[0], *across)
+    column = add(own, *across)
     routed_out = add(
         column[:count],
         *[swap(column[k * count : (k + 1) * count], k, 0) for k in range(1, side)],

time: 49.9 us -> 48.5 us (0.972)
  starting transfers between devices: 13.9 us -> 12.1 us
    ppermute x6, starting transfers between devices: 10.1 us -> 9.23 us  [swap(): return lax.ppermute(x, 'side', [(i, i ^ side_bits) for i in range(side)])]
    ppermute x6, waiting for transfers between devices: 4.55 us -> 5.41 us  [swap(): return lax.ppermute(x, 'side', [(i, i ^ side_bits) for i in range(side)])]
    ppermute x5 -> x6, starting transfers between devices: 3.73 us -> 2.88 us  [swap(): return lax.ppermute(x, 'dev', [(i, i ^ dev_bits) for i in range(dev)])]
    ppermute x5 -> x6, waiting for transfers between devices: 5.33 us -> 4.5 us  [swap(): return lax.ppermute(x, 'dev', [(i, i ^ dev_bits) for i in range(dev)])]
    pallas_call x3 -> x4, Pallas kernels: 19.2 us -> 19.4 us  [the longest x3 11.6 us: fetch(): pl.pallas_call(functools.partial(fetch_kernel, e, first), out_shape=pltpu...]
  transfers between devices with their start and end apart: 11 -> 12, of which waited for: 8 -> 5; matrix products, arithmetic and copies ran while one was open for 0% -> 0% of each run, Pallas kernels for 31% -> 32%
where the time goes in v3:
time: 48.5 us; the launch traced here: 48.4 us
  Pallas kernels  24.5 us (51%)
  starting transfers between devices  12.1 us (25%)
  waiting for transfers between devices  9.91 us (20%)
  other arithmetic  0.97 us (2%)
  between operations  0.8 us (2%)
    pallas_call x3, Pallas kernels, fetch(): pl.pallas_call(functools.partial(fetch_kernel, e, first), out_shape=pltpu...  11.6 us
    ppermute x6, starting transfers between devices, swap(): return lax.ppermute(x, 'side', [(i, i ^ side_bits) for i in range(side)])  9.23 us
    pallas_call x1, Pallas kernels, run_experts(): pl.pallas_call(functools.partial(experts_kernel, len(parts), tuple((len(x...  7.82 us
    ppermute x6, waiting for transfers between devices, swap(): return lax.ppermute(x, 'side', [(i, i ^ side_bits) for i in range(side)])  5.41 us
    ppermute x6, waiting for transfers between devices, swap(): return lax.ppermute(x, 'dev', [(i, i ^ dev_bits) for i in range(dev)])  4.5 us
    pallas_call x1, Pallas kernels, attend(): pl.pallas_call(attend_kernel, out_shape=pltpu.HBM(query_latent.shape, BF1...  4 us
    ppermute x6, starting transfers between devices, swap(): return lax.ppermute(x, 'dev', [(i, i ^ dev_bits) for i in range(dev)])  2.88 us
    pallas_call x1, Pallas kernels, pack(): pl.pallas_call(pack_kernel, out_shape=pltpu.VMEM((rows, width + pad), BF1...  1.08 us
  transfers between devices with their start and end apart: 12, of which 5 were waited for; matrix products, arithmetic and copies ran while one was open for 0% of the time, Pallas kernels for 32%

profile of v3, /device:TPU:0, one launch (start us, length us, event | category | flops | bytes accessed | tf_op | source)
XLA Modules:
  0.0 48.4 jit_solution(13618319525726810490)
XLA Ops:
  0.6 0.0 slice-start
  0.6 1.1 %pack.1 = bf16[4,7296]{1,0:T(4,128)(2,1)S(1)} custom-call(bf16[4,7168]{1,0:T(4,128)(2,1)} %tokens.1, s32[4,4]{1,0:T(4,128)} %routes.1, bf16[4,4]{1,0:T(4,128)(2,1)} %gates.1), custom_call_target="tpu_custom_call" | custom-call | tf_op jit(solution)/shard_map/pack/pallas_call | solution.py:60
  1.7 0.0 slice-start.1
  1.7 0.0 slice-start.2
  1.8 0.0 slice-start.3
  1.8 3.1 %collective-permute-start = (bf16[4,7296]{1,0:T(4,128)(2,1)S(1)}, bf16[4,7296]{1,0:T(4,128)(2,1)S(1)}, u32[]{:S(2)}, u32[]{:S(2)}) collective-permute-start(bf16[4,7296]{1,0:T(4,128)(2,1)S(1)} %pack.1), channel_id=1, source_target_pairs={{0,4},{4,0},{8,12},{12,8},{1,5},{5,1},{9,13},{13,9},{2,6},{6,2},{1... | collective-permute-start | bytes 175112 | tf_op jit(solution)/shard_map/ppermute | solution.py:21
  4.9 2.6 %collective-permute-start.1 = (bf16[4,7296]{1,0:T(4,128)(2,1)S(1)}, bf16[4,7296]{1,0:T(4,128)(2,1)S(1)}, u32[]{:S(2)}, u32[]{:S(2)}) collective-permute-start(bf16[4,7296]{1,0:T(4,128)(2,1)S(1)} %pack.1), channel_id=1, source_target_pairs={{0,8},{4,12},{8,0},{12,4},{1,9},{5,13},{9,1},{13,5},{2,10},{6,14},... | collective-permute-start | bytes 175112 | tf_op jit(solution)/shard_map/ppermute | solution.py:21
  7.4 0.0 collective-permute-start.2
  7.5 4.7 %fetch.3.refs_4_ = bf16[2,6144,512]{2,1,0:T(8,128)(2,1)S(1)} custom-call(bf16[2,2,7168,512]{3,2,1,0:T(8,128)(2,1)} %w_in.4), custom_call_target="tpu_custom_call" | custom-call | tf_op jit(solution)/shard_map/fetch/pallas_call | solution.py:95
  12.2 0.0 collective-permute-done
  12.2 0.0 collective-permute-done.1
  12.2 1.3 %collective-permute-done.2 = bf16[4,7296]{1,0:T(4,128)(2,1)S(1)} collective-permute-done((bf16[4,7296]{1,0:T(4,128)(2,1)S(1)}, bf16[4,7296]{1,0:T(4,128)(2,1)S(1)}, u32[]{:S(2)}, u32[]{:S(2)}) %collective-permute-start.2) | collective-permute-done | bytes 58400 | tf_op jit(solution)/shard_map/ppermute | solution.py:21
  13.4 0.1 pad_maximum_fusion.refs_0_
  13.6 1.6 %collective-permute-start.3 = (bf16[16,7296]{1,0:T(8,128)(2,1)S(1)}, bf16[16,7296]{1,0:T(8,128)(2,1)S(1)}, u32[]{:S(2)}, u32[]{:S(2)}) collective-permute-start(bf16[16,7296]{1,0:T(8,128)(2,1)S(1)} %pad_maximum_fusion.refs_0_), channel_id=1, source_target_pairs={{0,2},{1,3},{2,0},{3,1},{4,6},{5,7},{6,4},{7,5},{8,10},{9,11},{10,... | collective-permute-start | bytes 700424 | tf_op jit(solution)/shard_map/ppermute | solution.py:19
  15.1 0.0 slice-done
  15.1 0.0 slice-done.1
  15.1 0.0 slice-done.2
  15.1 0.0 slice-done.3
  15.2 5.3 %fetch.4.refs_6_ = bf16[2,7168,512]{2,1,0:T(8,128)(2,1)S(1)} custom-call(bf16[2,2,7168,512]{3,2,1,0:T(8,128)(2,1)} %w_in.4, bf16[2,512,7168]{2,1,0:T(8,128)(2,1)S(1)} %bitcast.1), custom_call_target="tpu_custom_call" | custom-call | tf_op jit(solution)/shard_map/fetch/pallas_call | solution.py:95
  20.5 0.1 collective-permute-start.4
  20.6 0.0 collective-permute-done.3.refs_1_
  20.6 0.5 %collective-permute-start.5 = (bf16[16,7296]{1,0:T(8,128)(2,1)S(1)}, bf16[16,7296]{1,0:T(8,128)(2,1)S(1)}, u32[]{:S(2)}, u32[]{:S(2)}) collective-permute-start(bf16[16,7296]{1,0:T(8,128)(2,1)S(1)} %collective-permute-done.3.refs_1_), channel_id=1, source_target_pairs={{0,1},{1,0},{2,3},{3,2},{4,5},{5,4},{6,7},{7,6},{8,9},{9,8},{10,11... | collective-permute-start | bytes 700424 | tf_op jit(solution)/shard_map/ppermute | solution.py:19
  21.1 1.6 %fetch.5.refs_5_ = bf16[2,1024,512]{2,1,0:T(8,128)(2,1)S(1)} custom-call(bf16[2,2,7168,512]{3,2,1,0:T(8,128)(2,1)} %w_in.4), custom_call_target="tpu_custom_call" | custom-call | tf_op jit(solution)/shard_map/fetch/pallas_call | solution.py:95
  22.6 0.0 collective-permute-done.4.refs_2_
  22.6 0.0 collective-permute-done.5.refs_3_
  22.7 7.8 %experts.1 = (bf16[16,7168]{1,0:T(8,128)(2,1)S(1)}, bf16[16,7168]{1,0:T(8,128)(2,1)S(1)}, bf16[16,7168]{1,0:T(8,128)(2,1)S(1)}, bf16[16,7168]{1,0:T(8,128)(2,1)S(1)}) custom-call(bf16[16,7296]{1,0:T(8,128)(2,1)S(1)} %pad_maximum_fusion.refs_0_, bf16[16,7296]{1,0:T(8,128)(2,1)S(1)} %collective-permute-done.3.refs_1_, ...), custom_call_target="tpu_custom_call" | custom-call | flops 2818572288 | bytes 44040192 | tf_op jit(solution)/shard_map/experts/pallas_call | solution.py:204
  30.5 0.2 collective-permute-start.6
  30.6 1.4 %collective-permute-done.6 = bf16[16,7168]{1,0:T(8,128)(2,1)S(1)} collective-permute-done((bf16[16,7168]{1,0:T(8,128)(2,1)S(1)}, bf16[16,7168]{1,0:T(8,128)(2,1)S(1)}, u32[]{:S(2)}, u32[]{:S(2)}) %collective-permute-start.6) | collective-permute-done | bytes 229408 | tf_op jit(solution)/shard_map/ppermute | solution.py:19
  32.0 0.1 add_convert_fusion.2
  32.1 0.6 %collective-permute-start.8 = (bf16[16,7168]{1,0:T(8,128)(2,1)S(1)}, bf16[16,7168]{1,0:T(8,128)(2,1)S(1)}, u32[]{:S(2)}, u32[]{:S(2)}) collective-permute-start(bf16[16,7168]{1,0:T(8,128)(2,1)S(1)} %add_convert_fusion.2), channel_id=1, source_target_pairs={{0,2},{1,3},{2,0},{3,1},{4,6},{5,7},{6,4},{7,5},{8,10},{9,11},{10,... | collective-permute-start | bytes 688136 | tf_op jit(solution)/shard_map/ppermute | solution.py:19
  32.7 0.0 collective-permute-start.7
  32.7 4.0 %attend.1 = bf16[2,128,512]{2,1,0:T(8,128)(2,1)} custom-call(s32[2]{0:T(128)} %lengths.1, bf16[2,128,512]{2,1,0:T(8,128)(2,1)} %queries.1, bf16[2,64,128]{2,1,0:T(8,128)(2,1)} %rope_queries.1, bf16[2,512,512]{2,1,0:T(8,128)(2,1)} %latents.1, bf16[2,64,512]{2,1,0:T(8,128)(2,1)} %ropes.1), custom_call_target="tpu_custom_call" | custom-call | tf_op jit(solution)/shard_map/attend/pallas_call | solution.py:139
  36.7 3.1 %collective-permute-done.8 = bf16[16,7168]{1,0:T(8,128)(2,1)S(1)} collective-permute-done((bf16[16,7168]{1,0:T(8,128)(2,1)S(1)}, bf16[16,7168]{1,0:T(8,128)(2,1)S(1)}, u32[]{:S(2)}, u32[]{:S(2)}) %collective-permute-start.8) | collective-permute-done | bytes 229408 | tf_op jit(solution)/shard_map/ppermute | solution.py:19
  39.8 0.0 collective-permute-done.7
  39.8 0.1 add_convert_fusion
  39.9 0.1 fusion
  40.0 1.1 %collective-permute-start.10 = (bf16[4,7168]{1,0:T(4,128)(2,1)S(1)}, bf16[4,7168]{1,0:T(4,128)(2,1)S(1)}, u32[]{:S(2)}, u32[]{:S(2)}) collective-permute-start(bf16[4,7168]{1,0:T(4,128)(2,1)S(1)} %get-tuple-element.42), channel_id=1, source_target_pairs={{0,8},{4,12},{8,0},{12,4},{1,9},{5,13},{9,1},{13,5},{2,10},{6,14},... | collective-permute-start | bytes 172040 | tf_op jit(solution)/shard_map/ppermute | solution.py:21
  41.1 1.6 %collective-permute-start.11 = (bf16[4,7168]{1,0:T(4,128)(2,1)S(1)}, bf16[4,7168]{1,0:T(4,128)(2,1)S(1)}, u32[]{:S(2)}, u32[]{:S(2)}) collective-permute-start(bf16[4,7168]{1,0:T(4,128)(2,1)S(1)} %get-tuple-element.41), channel_id=1, source_target_pairs={{0,12},{4,8},{8,4},{12,0},{1,13},{5,9},{9,5},{13,1},{2,14},{6,10},... | collective-permute-start | bytes 172040 | tf_op jit(solution)/shard_map/ppermute | solution.py:21
  42.7 0.8 %collective-permute-start.9 = (bf16[4,7168]{1,0:T(4,128)(2,1)S(1)}, bf16[4,7168]{1,0:T(4,128)(2,1)S(1)}, u32[]{:S(2)}, u32[]{:S(2)}) collective-permute-start(bf16[4,7168]{1,0:T(4,128)(2,1)S(1)} %get-tuple-element.40), channel_id=1, source_target_pairs={{0,4},{4,0},{8,12},{12,8},{1,5},{5,1},{9,13},{13,9},{2,6},{6,2},{1... | collective-permute-start | bytes 172040 | tf_op jit(solution)/shard_map/ppermute | solution.py:21
  43.5 3.7 %collective-permute-done.10 = bf16[4,7168]{1,0:T(4,128)(2,1)S(1)} collective-permute-done((bf16[4,7168]{1,0:T(4,128)(2,1)S(1)}, bf16[4,7168]{1,0:T(4,128)(2,1)S(1)}, u32[]{:S(2)}, u32[]{:S(2)}) %collective-permute-start.10) | collective-permute-done | bytes 57376 | tf_op jit(solution)/shard_map/ppermute | solution.py:21
  47.3 0.0 collective-permute-done.11
  47.3 0.4 collective-permute-done.9
  47.7 0.7 %add_convert_fusion.3 = bf16[4,7168]{1,0:T(4,128)(2,1)} fusion(bf16[4,7168]{1,0:T(4,128)(2,1)S(1)} %collective-permute-done.11, bf16[4,7168]{1,0:T(4,128)(2,1)S(1)} %collective-permute-done.10, bf16[4,7168]{1,0:T(4,128)(2,1)S(1)} %collective-permute-done.9, bf16[16,7168]{1,0:T(8,128)(2,1)S(1)} %add_convert_fusion), kind=kLoop, calls=%fused_computation.4 | loop fusion | flops 229376 | bytes 286720 | tf_op jit(solution)/shard_map/convert_element_type | solution.py:226
  (1 shorter events, 0.0 us)
Async XLA Ops:
  0.6 14.5 %slice-start = ((s8[14680064]{0:T(1024)(128)(4,1)}), s8[4194304]{0:T(1024)(128)(4,1)S(1)}, s32[]{:S(2)}) async-start(s8[14680064]{0:T(1024)(128)(4,1)} %bitcast), calls=%async_computation | async-start | bytes 8388608
  1.7 13.4 %slice-start.1 = ((s8[14680064]{0:T(1024)(128)(4,1)}), s8[4194304]{0:T(1024)(128)(4,1)S(1)}, s32[]{:S(2)}) async-start(s8[14680064]{0:T(1024)(128)(4,1)} %bitcast), calls=%async_computation.1 | async-start | bytes 8388608
  1.7 13.4 %slice-start.2 = ((s8[14680064]{0:T(1024)(128)(4,1)}), s8[4194304]{0:T(1024)(128)(4,1)S(1)}, s32[]{:S(2)}) async-start(s8[14680064]{0:T(1024)(128)(4,1)} %bitcast), calls=%async_computation.2 | async-start | bytes 8388608
  1.8 13.4 %slice-start.3 = ((s8[14680064]{0:T(1024)(128)(4,1)}), s8[2097152]{0:T(1024)(128)(4,1)S(1)}, s32[]{:S(2)}) async-start(s8[14680064]{0:T(1024)(128)(4,1)} %bitcast), calls=%async_computation.3 | async-start | bytes 4194304
  1.8 10.4 %collective-permute-start = (bf16[4,7296]{1,0:T(4,128)(2,1)S(1)}, bf16[4,7296]{1,0:T(4,128)(2,1)S(1)}, u32[]{:S(2)}, u32[]{:S(2)}) collective-permute-start(bf16[4,7296]{1,0:T(4,128)(2,1)S(1)} %pack.1), channel_id=1, source_target_pairs={{0,4},{4,0},{8,12},{12,8},{1,5},{5,1},{9,13},{13,9},{2,6},{6,2},{1... | collective-permute-start | bytes 175112 | tf_op jit(solution)/shard_map/ppermute | solution.py:21
  4.9 7.3 %collective-permute-start.1 = (bf16[4,7296]{1,0:T(4,128)(2,1)S(1)}, bf16[4,7296]{1,0:T(4,128)(2,1)S(1)}, u32[]{:S(2)}, u32[]{:S(2)}) collective-permute-start(bf16[4,7296]{1,0:T(4,128)(2,1)S(1)} %pack.1), channel_id=1, source_target_pairs={{0,8},{4,12},{8,0},{12,4},{1,9},{5,13},{9,1},{13,5},{2,10},{6,14},... | collective-permute-start | bytes 175112 | tf_op jit(solution)/shard_map/ppermute | solution.py:21
  7.4 6.0 %collective-permute-start.2 = (bf16[4,7296]{1,0:T(4,128)(2,1)S(1)}, bf16[4,7296]{1,0:T(4,128)(2,1)S(1)}, u32[]{:S(2)}, u32[]{:S(2)}) collective-permute-start(bf16[4,7296]{1,0:T(4,128)(2,1)S(1)} %pack.1), channel_id=1, source_target_pairs={{0,12},{4,8},{8,4},{12,0},{1,13},{5,9},{9,5},{13,1},{2,14},{6,10},... | collective-permute-start | bytes 175112 | tf_op jit(solution)/shard_map/ppermute | solution.py:21
  13.6 7.0 %collective-permute-start.3 = (bf16[16,7296]{1,0:T(8,128)(2,1)S(1)}, bf16[16,7296]{1,0:T(8,128)(2,1)S(1)}, u32[]{:S(2)}, u32[]{:S(2)}) collective-permute-start(bf16[16,7296]{1,0:T(8,128)(2,1)S(1)} %pad_maximum_fusion.refs_0_), channel_id=1, source_target_pairs={{0,2},{1,3},{2,0},{3,1},{4,6},{5,7},{6,4},{7,5},{8,10},{9,11},{10,... | collective-permute-start | bytes 700424 | tf_op jit(solution)/shard_map/ppermute | solution.py:19
  20.5 2.1 %collective-permute-start.4 = (bf16[16,7296]{1,0:T(8,128)(2,1)S(1)}, bf16[16,7296]{1,0:T(8,128)(2,1)S(1)}, u32[]{:S(2)}, u32[]{:S(2)}) collective-permute-start(bf16[16,7296]{1,0:T(8,128)(2,1)S(1)} %pad_maximum_fusion.refs_0_), channel_id=1, source_target_pairs={{0,1},{1,0},{2,3},{3,2},{4,5},{5,4},{6,7},{7,6},{8,9},{9,8},{10,11... | collective-permute-start | bytes 700424 | tf_op jit(solution)/shard_map/ppermute | solution.py:19
  20.6 2.1 %collective-permute-start.5 = (bf16[16,7296]{1,0:T(8,128)(2,1)S(1)}, bf16[16,7296]{1,0:T(8,128)(2,1)S(1)}, u32[]{:S(2)}, u32[]{:S(2)}) collective-permute-start(bf16[16,7296]{1,0:T(8,128)(2,1)S(1)} %collective-permute-done.3.refs_1_), channel_id=1, source_target_pairs={{0,1},{1,0},{2,3},{3,2},{4,5},{5,4},{6,7},{7,6},{8,9},{9,8},{10,11... | collective-permute-start | bytes 700424 | tf_op jit(solution)/shard_map/ppermute | solution.py:19
  30.5 1.6 %collective-permute-start.6 = (bf16[16,7168]{1,0:T(8,128)(2,1)S(1)}, bf16[16,7168]{1,0:T(8,128)(2,1)S(1)}, u32[]{:S(2)}, u32[]{:S(2)}) collective-permute-start(bf16[16,7168]{1,0:T(8,128)(2,1)S(1)} %get-tuple-element.35), channel_id=1, source_target_pairs={{0,1},{1,0},{2,3},{3,2},{4,5},{5,4},{6,7},{7,6},{8,9},{9,8},{10,11... | collective-permute-start | bytes 688136 | tf_op jit(solution)/shard_map/ppermute | solution.py:19
  32.1 7.7 %collective-permute-start.8 = (bf16[16,7168]{1,0:T(8,128)(2,1)S(1)}, bf16[16,7168]{1,0:T(8,128)(2,1)S(1)}, u32[]{:S(2)}, u32[]{:S(2)}) collective-permute-start(bf16[16,7168]{1,0:T(8,128)(2,1)S(1)} %add_convert_fusion.2), channel_id=1, source_target_pairs={{0,2},{1,3},{2,0},{3,1},{4,6},{5,7},{6,4},{7,5},{8,10},{9,11},{10,... | collective-permute-start | bytes 688136 | tf_op jit(solution)/shard_map/ppermute | solution.py:19
  32.7 7.1 %collective-permute-start.7 = (bf16[16,7168]{1,0:T(8,128)(2,1)S(1)}, bf16[16,7168]{1,0:T(8,128)(2,1)S(1)}, u32[]{:S(2)}, u32[]{:S(2)}) collective-permute-start(bf16[16,7168]{1,0:T(8,128)(2,1)S(1)} %get-tuple-element.36), channel_id=1, source_target_pairs={{0,1},{1,0},{2,3},{3,2},{4,5},{5,4},{6,7},{7,6},{8,9},{9,8},{10,11... | collective-permute-start | bytes 688136 | tf_op jit(solution)/shard_map/ppermute | solution.py:19
  40.0 7.3 %collective-permute-start.10 = (bf16[4,7168]{1,0:T(4,128)(2,1)S(1)}, bf16[4,7168]{1,0:T(4,128)(2,1)S(1)}, u32[]{:S(2)}, u32[]{:S(2)}) collective-permute-start(bf16[4,7168]{1,0:T(4,128)(2,1)S(1)} %get-tuple-element.42), channel_id=1, source_target_pairs={{0,8},{4,12},{8,0},{12,4},{1,9},{5,13},{9,1},{13,5},{2,10},{6,14},... | collective-permute-start | bytes 172040 | tf_op jit(solution)/shard_map/ppermute | solution.py:21
  41.1 6.2 %collective-permute-start.11 = (bf16[4,7168]{1,0:T(4,128)(2,1)S(1)}, bf16[4,7168]{1,0:T(4,128)(2,1)S(1)}, u32[]{:S(2)}, u32[]{:S(2)}) collective-permute-start(bf16[4,7168]{1,0:T(4,128)(2,1)S(1)} %get-tuple-element.41), channel_id=1, source_target_pairs={{0,12},{4,8},{8,4},{12,0},{1,13},{5,9},{9,5},{13,1},{2,14},{6,10},... | collective-permute-start | bytes 172040 | tf_op jit(solution)/shard_map/ppermute | solution.py:21
  42.7 5.0 %collective-permute-start.9 = (bf16[4,7168]{1,0:T(4,128)(2,1)S(1)}, bf16[4,7168]{1,0:T(4,128)(2,1)S(1)}, u32[]{:S(2)}, u32[]{:S(2)}) collective-permute-start(bf16[4,7168]{1,0:T(4,128)(2,1)S(1)} %get-tuple-element.40), channel_id=1, source_target_pairs={{0,4},{4,0},{8,12},{12,8},{1,5},{5,1},{9,13},{13,9},{2,6},{6,2},{1... | collective-permute-start | bytes 172040 | tf_op jit(solution)/shard_map/ppermute | solution.py:21

commit v4 on v3

--- a/solution.py
+++ b/solution.py
@@ -36,21 +36,21 @@
 MIB = 1024 * 1024
 
 
-def pack_kernel(tokens, routes, gates, out, tokens_here, routes_here, gates_here, sems):
-    pairs = ((tokens, tokens_here), (routes, routes_here), (gates, gates_here))
+def pack_kernel(tokens, routes, gates, out, routes_here, gates_here, sems):
+    width = tokens.shape[1]
+    pairs = ((tokens, out.at[:, :width]), (routes, routes_here), (gates, gates_here))
     copies = [pltpu.make_async_copy(a, b, sems.at[i]) for i, (a, b) in enumerate(pairs)]
     for copy in copies:
         copy.start()
-    for copy in copies:
+    for copy in copies[1:]:
         copy.wait()
-    width = tokens.shape[1]
-    out[:, :width] = tokens_here[...]
     lane = lax.broadcasted_iota(jnp.int32, (tokens.shape[0], out.shape[1] - width), 1)
     total = jnp.zeros(lane.shape, F32)
     gate = gates_here[...].astype(F32)
     for k in range(routes.shape[1]):
         total = total + jnp.where(routes_here[:, k : k + 1] == lane, gate[:, k : k + 1], 0.0)
     out[:, width:] = total.astype(BF16)
+    copies[0].wait()
 
 
 def pack(tokens, routes, gates, experts):
@@ -62,7 +62,7 @@
         out_shape=pltpu.VMEM((rows, width + pad), BF16),
         in_specs=[HBM] * 3,
         out_specs=VMEM,
-        scratch_shapes=[pltpu.VMEM(x.shape, x.dtype) for x in arrays] + [pltpu.SemaphoreType.DMA((3,))],
+        scratch_shapes=[pltpu.VMEM(x.shape, x.dtype) for x in arrays[1:]] + [pltpu.SemaphoreType.DMA((3,))],
         compiler_params=pltpu.CompilerParams(vmem_limit_bytes=2 * MIB),
         name="pack",
     )(*[in_hbm(x) for x in arrays])
@@ -244,9 +244,11 @@
     packed = pack(tokens, routes, gate_weights, experts_in.shape[0] * side)
     chunks = chunks_of(tokens.shape[1])[1]
     last = 1 if chunks > 2 else 0
-    along = [packed] + [swap(packed, k, 0) for k in range(1, side)]
+    order = [*range(2, side), 1]
+    along = [swap(packed, k, 0) for k in order]
     first = fetch(experts_in, 0, 0, chunks - last)
     *along, first = lax.optimization_barrier((*along, first))
+    along = [packed] + [along[order.index(k)] for k in range(1, side)]
     along = jnp.concatenate(along)
     near = [along] + [swap(along, 0, 2 * k) for k in range(1, chips)]
     others = [fetch(experts_in, e, 0, chunks, experts_out) for e in range(1, experts_in.shape[0])]

time: 48.5 us -> 48.5 us (level)
  starting transfers between devices: 12.1 us -> 13.4 us
  waiting for transfers between devices: 9.91 us -> 8.67 us
    ppermute x6, starting transfers between devices: 9.23 us -> 9.91 us  [swap(): return lax.ppermute(x, 'side', [(i, i ^ side_bits) for i in range(side)])]
    ppermute x6, starting transfers between devices: 2.88 us -> 3.51 us  [swap(): return lax.ppermute(x, 'dev', [(i, i ^ dev_bits) for i in range(dev)])]
    ppermute x6, waiting for transfers between devices: 4.5 us -> 3.87 us  [swap(): return lax.ppermute(x, 'dev', [(i, i ^ dev_bits) for i in range(dev)])]
    ppermute x6, waiting for transfers between devices: 5.41 us -> 4.8 us  [swap(): return lax.ppermute(x, 'side', [(i, i ^ side_bits) for i in range(side)])]
where the time goes in v4:
time: 48.5 us; the launch traced here: 48.3 us
  Pallas kernels  24.4 us (50%)
  starting transfers between devices  13.4 us (28%)
  waiting for transfers between devices  8.67 us (18%)
  other arithmetic  0.97 us (2%)
  between operations  0.81 us (2%)
    pallas_call x3, Pallas kernels, fetch(): pl.pallas_call(functools.partial(fetch_kernel, e, first), out_shape=pltpu...  11.6 us
    ppermute x6, starting transfers between devices, swap(): return lax.ppermute(x, 'side', [(i, i ^ side_bits) for i in range(side)])  9.91 us
    pallas_call x1, Pallas kernels, run_experts(): pl.pallas_call(functools.partial(experts_kernel, len(parts), tuple((len(x...  7.82 us
    ppermute x6, waiting for transfers between devices, swap(): return lax.ppermute(x, 'side', [(i, i ^ side_bits) for i in range(side)])  4.8 us
    pallas_call x1, Pallas kernels, attend(): pl.pallas_call(attend_kernel, out_shape=pltpu.HBM(query_latent.shape, BF1...  4 us
    ppermute x6, waiting for transfers between devices, swap(): return lax.ppermute(x, 'dev', [(i, i ^ dev_bits) for i in range(dev)])  3.87 us
    ppermute x6, starting transfers between devices, swap(): return lax.ppermute(x, 'dev', [(i, i ^ dev_bits) for i in range(dev)])  3.51 us
    pallas_call x1, Pallas kernels, pack(): pl.pallas_call(pack_kernel, out_shape=pltpu.VMEM((rows, width + pad), BF1...  1 us
  transfers between devices with their start and end apart: 12, of which 5 were waited for; matrix products, arithmetic and copies ran while one was open for 0% of the time, Pallas kernels for 32%

profile of v4, /device:TPU:0, one launch (start us, length us, event | category | flops | bytes accessed | tf_op | source)
XLA Modules:
  0.0 48.3 jit_solution(12308219624741894370)
XLA Ops:
  0.6 0.0 slice-start
  0.6 1.0 %pack.1 = bf16[4,7296]{1,0:T(4,128)(2,1)S(1)} custom-call(bf16[4,7168]{1,0:T(4,128)(2,1)} %tokens.1, s32[4,4]{1,0:T(4,128)} %routes.1, bf16[4,4]{1,0:T(4,128)(2,1)} %gates.1), custom_call_target="tpu_custom_call" | custom-call | tf_op jit(solution)/shard_map/pack/pallas_call | solution.py:60
  1.6 0.0 slice-start.1
  1.7 0.0 slice-start.2
  1.7 0.0 slice-start.3
  1.7 4.1 %collective-permute-start = (bf16[4,7296]{1,0:T(4,128)(2,1)S(1)}, bf16[4,7296]{1,0:T(4,128)(2,1)S(1)}, u32[]{:S(2)}, u32[]{:S(2)}) collective-permute-start(bf16[4,7296]{1,0:T(4,128)(2,1)S(1)} %pack.1), channel_id=1, source_target_pairs={{0,8},{4,12},{8,0},{12,4},{1,9},{5,13},{9,1},{13,5},{2,10},{6,14},... | collective-permute-start | bytes 175112 | tf_op jit(solution)/shard_map/ppermute | solution.py:21
  5.8 1.3 %collective-permute-start.1 = (bf16[4,7296]{1,0:T(4,128)(2,1)S(1)}, bf16[4,7296]{1,0:T(4,128)(2,1)S(1)}, u32[]{:S(2)}, u32[]{:S(2)}) collective-permute-start(bf16[4,7296]{1,0:T(4,128)(2,1)S(1)} %pack.1), channel_id=1, source_target_pairs={{0,12},{4,8},{8,4},{12,0},{1,13},{5,9},{9,5},{13,1},{2,14},{6,10},... | collective-permute-start | bytes 175112 | tf_op jit(solution)/shard_map/ppermute | solution.py:21
  7.1 0.2 collective-permute-start.2
  7.4 4.7 %fetch.3.refs_4_ = bf16[2,6144,512]{2,1,0:T(8,128)(2,1)S(1)} custom-call(bf16[2,2,7168,512]{3,2,1,0:T(8,128)(2,1)} %w_in.4), custom_call_target="tpu_custom_call" | custom-call | tf_op jit(solution)/shard_map/fetch/pallas_call | solution.py:95
  12.1 0.0 collective-permute-done
  12.1 0.0 collective-permute-done.1
  12.1 0.0 collective-permute-done.2
  12.1 0.1 pad_maximum_fusion.refs_0_
  12.3 1.6 %collective-permute-start.3 = (bf16[16,7296]{1,0:T(8,128)(2,1)S(1)}, bf16[16,7296]{1,0:T(8,128)(2,1)S(1)}, u32[]{:S(2)}, u32[]{:S(2)}) collective-permute-start(bf16[16,7296]{1,0:T(8,128)(2,1)S(1)} %pad_maximum_fusion.refs_0_), channel_id=1, source_target_pairs={{0,2},{1,3},{2,0},{3,1},{4,6},{5,7},{6,4},{7,5},{8,10},{9,11},{10,... | collective-permute-start | bytes 700424 | tf_op jit(solution)/shard_map/ppermute | solution.py:19
  13.8 0.0 slice-done
  13.8 0.0 slice-done.1
  13.8 0.0 slice-done.2
  13.8 0.0 slice-done.3
  13.8 5.3 %fetch.4.refs_6_ = bf16[2,7168,512]{2,1,0:T(8,128)(2,1)S(1)} custom-call(bf16[2,2,7168,512]{3,2,1,0:T(8,128)(2,1)} %w_in.4, bf16[2,512,7168]{2,1,0:T(8,128)(2,1)S(1)} %bitcast.1), custom_call_target="tpu_custom_call" | custom-call | tf_op jit(solution)/shard_map/fetch/pallas_call | solution.py:95
  19.2 0.1 collective-permute-start.4
  19.2 0.0 collective-permute-done.3.refs_1_
  19.2 0.5 %collective-permute-start.5 = (bf16[16,7296]{1,0:T(8,128)(2,1)S(1)}, bf16[16,7296]{1,0:T(8,128)(2,1)S(1)}, u32[]{:S(2)}, u32[]{:S(2)}) collective-permute-start(bf16[16,7296]{1,0:T(8,128)(2,1)S(1)} %collective-permute-done.3.refs_1_), channel_id=1, source_target_pairs={{0,1},{1,0},{2,3},{3,2},{4,5},{5,4},{6,7},{7,6},{8,9},{9,8},{10,11... | collective-permute-start | bytes 700424 | tf_op jit(solution)/shard_map/ppermute | solution.py:19
  19.7 1.6 %fetch.5.refs_5_ = bf16[2,1024,512]{2,1,0:T(8,128)(2,1)S(1)} custom-call(bf16[2,2,7168,512]{3,2,1,0:T(8,128)(2,1)} %w_in.4), custom_call_target="tpu_custom_call" | custom-call | tf_op jit(solution)/shard_map/fetch/pallas_call | solution.py:95
  21.3 0.0 collective-permute-done.4.refs_2_
  21.3 0.0 collective-permute-done.5.refs_3_
  21.3 7.8 %experts.1 = (bf16[16,7168]{1,0:T(8,128)(2,1)S(1)}, bf16[16,7168]{1,0:T(8,128)(2,1)S(1)}, bf16[16,7168]{1,0:T(8,128)(2,1)S(1)}, bf16[16,7168]{1,0:T(8,128)(2,1)S(1)}) custom-call(bf16[16,7296]{1,0:T(8,128)(2,1)S(1)} %pad_maximum_fusion.refs_0_, bf16[16,7296]{1,0:T(8,128)(2,1)S(1)} %collective-permute-done.3.refs_1_, ...), custom_call_target="tpu_custom_call" | custom-call | flops 2818572288 | bytes 44040192 | tf_op jit(solution)/shard_map/experts/pallas_call | solution.py:204
  29.1 0.2 collective-permute-start.6
  29.3 1.4 %collective-permute-done.6 = bf16[16,7168]{1,0:T(8,128)(2,1)S(1)} collective-permute-done((bf16[16,7168]{1,0:T(8,128)(2,1)S(1)}, bf16[16,7168]{1,0:T(8,128)(2,1)S(1)}, u32[]{:S(2)}, u32[]{:S(2)}) %collective-permute-start.6) | collective-permute-done | bytes 229408 | tf_op jit(solution)/shard_map/ppermute | solution.py:19
  30.7 0.1 add_convert_fusion.2
  30.8 1.2 %collective-permute-start.8 = (bf16[16,7168]{1,0:T(8,128)(2,1)S(1)}, bf16[16,7168]{1,0:T(8,128)(2,1)S(1)}, u32[]{:S(2)}, u32[]{:S(2)}) collective-permute-start(bf16[16,7168]{1,0:T(8,128)(2,1)S(1)} %add_convert_fusion.2), channel_id=1, source_target_pairs={{0,2},{1,3},{2,0},{3,1},{4,6},{5,7},{6,4},{7,5},{8,10},{9,11},{10,... | collective-permute-start | bytes 688136 | tf_op jit(solution)/shard_map/ppermute | solution.py:19
  31.9 0.1 collective-permute-start.7
  32.0 4.0 %attend.1 = bf16[2,128,512]{2,1,0:T(8,128)(2,1)} custom-call(s32[2]{0:T(128)} %lengths.1, bf16[2,128,512]{2,1,0:T(8,128)(2,1)} %queries.1, bf16[2,64,128]{2,1,0:T(8,128)(2,1)} %rope_queries.1, bf16[2,512,512]{2,1,0:T(8,128)(2,1)} %latents.1, bf16[2,64,512]{2,1,0:T(8,128)(2,1)} %ropes.1), custom_call_target="tpu_custom_call" | custom-call | tf_op jit(solution)/shard_map/attend/pallas_call | solution.py:139
  36.0 2.5 %collective-permute-done.8 = bf16[16,7168]{1,0:T(8,128)(2,1)S(1)} collective-permute-done((bf16[16,7168]{1,0:T(8,128)(2,1)S(1)}, bf16[16,7168]{1,0:T(8,128)(2,1)S(1)}, u32[]{:S(2)}, u32[]{:S(2)}) %collective-permute-start.8) | collective-permute-done | bytes 229408 | tf_op jit(solution)/shard_map/ppermute | solution.py:19
  38.5 0.0 collective-permute-done.7
  38.5 0.1 add_convert_fusion
  38.6 0.1 fusion
  38.6 2.9 %collective-permute-start.10 = (bf16[4,7168]{1,0:T(4,128)(2,1)S(1)}, bf16[4,7168]{1,0:T(4,128)(2,1)S(1)}, u32[]{:S(2)}, u32[]{:S(2)}) collective-permute-start(bf16[4,7168]{1,0:T(4,128)(2,1)S(1)} %get-tuple-element.40), channel_id=1, source_target_pairs={{0,8},{4,12},{8,0},{12,4},{1,9},{5,13},{9,1},{13,5},{2,10},{6,14},... | collective-permute-start | bytes 172040 | tf_op jit(solution)/shard_map/ppermute | solution.py:21
  41.5 1.3 %collective-permute-start.11 = (bf16[4,7168]{1,0:T(4,128)(2,1)S(1)}, bf16[4,7168]{1,0:T(4,128)(2,1)S(1)}, u32[]{:S(2)}, u32[]{:S(2)}) collective-permute-start(bf16[4,7168]{1,0:T(4,128)(2,1)S(1)} %get-tuple-element.39), channel_id=1, source_target_pairs={{0,12},{4,8},{8,4},{12,0},{1,13},{5,9},{9,5},{13,1},{2,14},{6,10},... | collective-permute-start | bytes 172040 | tf_op jit(solution)/shard_map/ppermute | solution.py:21
  42.9 0.0 collective-permute-start.9
  42.9 2.9 %collective-permute-done.10 = bf16[4,7168]{1,0:T(4,128)(2,1)S(1)} collective-permute-done((bf16[4,7168]{1,0:T(4,128)(2,1)S(1)}, bf16[4,7168]{1,0:T(4,128)(2,1)S(1)}, u32[]{:S(2)}, u32[]{:S(2)}) %collective-permute-start.10) | collective-permute-done | bytes 57376 | tf_op jit(solution)/shard_map/ppermute | solution.py:21
  45.8 1.9 %collective-permute-done.11 = bf16[4,7168]{1,0:T(4,128)(2,1)S(1)} collective-permute-done((bf16[4,7168]{1,0:T(4,128)(2,1)S(1)}, bf16[4,7168]{1,0:T(4,128)(2,1)S(1)}, u32[]{:S(2)}, u32[]{:S(2)}) %collective-permute-start.11) | collective-permute-done | bytes 57376 | tf_op jit(solution)/shard_map/ppermute | solution.py:21
  47.6 0.1 collective-permute-done.9
  47.7 0.7 %add_convert_fusion.3 = bf16[4,7168]{1,0:T(4,128)(2,1)} fusion(bf16[4,7168]{1,0:T(4,128)(2,1)S(1)} %collective-permute-done.11, bf16[4,7168]{1,0:T(4,128)(2,1)S(1)} %collective-permute-done.10, bf16[4,7168]{1,0:T(4,128)(2,1)S(1)} %collective-permute-done.9, bf16[16,7168]{1,0:T(8,128)(2,1)S(1)} %add_convert_fusion), kind=kLoop, calls=%fused_computation.4 | loop fusion | flops 229376 | bytes 286720 | tf_op jit(solution)/shard_map/convert_element_type | solution.py:226
  (1 shorter events, 0.0 us)
Async XLA Ops:
  0.6 13.2 %slice-start = ((s8[14680064]{0:T(1024)(128)(4,1)}), s8[4194304]{0:T(1024)(128)(4,1)S(1)}, s32[]{:S(2)}) async-start(s8[14680064]{0:T(1024)(128)(4,1)} %bitcast), calls=%async_computation | async-start | bytes 8388608
  1.6 12.2 %slice-start.1 = ((s8[14680064]{0:T(1024)(128)(4,1)}), s8[4194304]{0:T(1024)(128)(4,1)S(1)}, s32[]{:S(2)}) async-start(s8[14680064]{0:T(1024)(128)(4,1)} %bitcast), calls=%async_computation.1 | async-start | bytes 8388608
  1.7 12.2 %slice-start.2 = ((s8[14680064]{0:T(1024)(128)(4,1)}), s8[4194304]{0:T(1024)(128)(4,1)S(1)}, s32[]{:S(2)}) async-start(s8[14680064]{0:T(1024)(128)(4,1)} %bitcast), calls=%async_computation.2 | async-start | bytes 8388608
  1.7 12.1 %slice-start.3 = ((s8[14680064]{0:T(1024)(128)(4,1)}), s8[2097152]{0:T(1024)(128)(4,1)S(1)}, s32[]{:S(2)}) async-start(s8[14680064]{0:T(1024)(128)(4,1)} %bitcast), calls=%async_computation.3 | async-start | bytes 4194304
  1.7 10.4 %collective-permute-start = (bf16[4,7296]{1,0:T(4,128)(2,1)S(1)}, bf16[4,7296]{1,0:T(4,128)(2,1)S(1)}, u32[]{:S(2)}, u32[]{:S(2)}) collective-permute-start(bf16[4,7296]{1,0:T(4,128)(2,1)S(1)} %pack.1), channel_id=1, source_target_pairs={{0,8},{4,12},{8,0},{12,4},{1,9},{5,13},{9,1},{13,5},{2,10},{6,14},... | collective-permute-start | bytes 175112 | tf_op jit(solution)/shard_map/ppermute | solution.py:21
  5.8 6.3 %collective-permute-start.1 = (bf16[4,7296]{1,0:T(4,128)(2,1)S(1)}, bf16[4,7296]{1,0:T(4,128)(2,1)S(1)}, u32[]{:S(2)}, u32[]{:S(2)}) collective-permute-start(bf16[4,7296]{1,0:T(4,128)(2,1)S(1)} %pack.1), channel_id=1, source_target_pairs={{0,12},{4,8},{8,4},{12,0},{1,13},{5,9},{9,5},{13,1},{2,14},{6,10},... | collective-permute-start | bytes 175112 | tf_op jit(solution)/shard_map/ppermute | solution.py:21
  7.1 5.0 %collective-permute-start.2 = (bf16[4,7296]{1,0:T(4,128)(2,1)S(1)}, bf16[4,7296]{1,0:T(4,128)(2,1)S(1)}, u32[]{:S(2)}, u32[]{:S(2)}) collective-permute-start(bf16[4,7296]{1,0:T(4,128)(2,1)S(1)} %pack.1), channel_id=1, source_target_pairs={{0,4},{4,0},{8,12},{12,8},{1,5},{5,1},{9,13},{13,9},{2,6},{6,2},{1... | collective-permute-start | bytes 175112 | tf_op jit(solution)/shard_map/ppermute | solution.py:21
  12.3 7.0 %collective-permute-start.3 = (bf16[16,7296]{1,0:T(8,128)(2,1)S(1)}, bf16[16,7296]{1,0:T(8,128)(2,1)S(1)}, u32[]{:S(2)}, u32[]{:S(2)}) collective-permute-start(bf16[16,7296]{1,0:T(8,128)(2,1)S(1)} %pad_maximum_fusion.refs_0_), channel_id=1, source_target_pairs={{0,2},{1,3},{2,0},{3,1},{4,6},{5,7},{6,4},{7,5},{8,10},{9,11},{10,... | collective-permute-start | bytes 700424 | tf_op jit(solution)/shard_map/ppermute | solution.py:19
  19.2 2.1 %collective-permute-start.4 = (bf16[16,7296]{1,0:T(8,128)(2,1)S(1)}, bf16[16,7296]{1,0:T(8,128)(2,1)S(1)}, u32[]{:S(2)}, u32[]{:S(2)}) collective-permute-start(bf16[16,7296]{1,0:T(8,128)(2,1)S(1)} %pad_maximum_fusion.refs_0_), channel_id=1, source_target_pairs={{0,1},{1,0},{2,3},{3,2},{4,5},{5,4},{6,7},{7,6},{8,9},{9,8},{10,11... | collective-permute-start | bytes 700424 | tf_op jit(solution)/shard_map/ppermute | solution.py:19
  19.2 2.1 %collective-permute-start.5 = (bf16[16,7296]{1,0:T(8,128)(2,1)S(1)}, bf16[16,7296]{1,0:T(8,128)(2,1)S(1)}, u32[]{:S(2)}, u32[]{:S(2)}) collective-permute-start(bf16[16,7296]{1,0:T(8,128)(2,1)S(1)} %collective-permute-done.3.refs_1_), channel_id=1, source_target_pairs={{0,1},{1,0},{2,3},{3,2},{4,5},{5,4},{6,7},{7,6},{8,9},{9,8},{10,11... | collective-permute-start | bytes 700424 | tf_op jit(solution)/shard_map/ppermute | solution.py:19
  29.1 1.6 %collective-permute-start.6 = (bf16[16,7168]{1,0:T(8,128)(2,1)S(1)}, bf16[16,7168]{1,0:T(8,128)(2,1)S(1)}, u32[]{:S(2)}, u32[]{:S(2)}) collective-permute-start(bf16[16,7168]{1,0:T(8,128)(2,1)S(1)} %get-tuple-element.33), channel_id=1, source_target_pairs={{0,1},{1,0},{2,3},{3,2},{4,5},{5,4},{6,7},{7,6},{8,9},{9,8},{10,11... | collective-permute-start | bytes 688136 | tf_op jit(solution)/shard_map/ppermute | solution.py:19
  30.8 7.7 %collective-permute-start.8 = (bf16[16,7168]{1,0:T(8,128)(2,1)S(1)}, bf16[16,7168]{1,0:T(8,128)(2,1)S(1)}, u32[]{:S(2)}, u32[]{:S(2)}) collective-permute-start(bf16[16,7168]{1,0:T(8,128)(2,1)S(1)} %add_convert_fusion.2), channel_id=1, source_target_pairs={{0,2},{1,3},{2,0},{3,1},{4,6},{5,7},{6,4},{7,5},{8,10},{9,11},{10,... | collective-permute-start | bytes 688136 | tf_op jit(solution)/shard_map/ppermute | solution.py:19
  31.9 6.6 %collective-permute-start.7 = (bf16[16,7168]{1,0:T(8,128)(2,1)S(1)}, bf16[16,7168]{1,0:T(8,128)(2,1)S(1)}, u32[]{:S(2)}, u32[]{:S(2)}) collective-permute-start(bf16[16,7168]{1,0:T(8,128)(2,1)S(1)} %get-tuple-element.34), channel_id=1, source_target_pairs={{0,1},{1,0},{2,3},{3,2},{4,5},{5,4},{6,7},{7,6},{8,9},{9,8},{10,11... | collective-permute-start | bytes 688136 | tf_op jit(solution)/shard_map/ppermute | solution.py:19
  38.6 7.1 %collective-permute-start.10 = (bf16[4,7168]{1,0:T(4,128)(2,1)S(1)}, bf16[4,7168]{1,0:T(4,128)(2,1)S(1)}, u32[]{:S(2)}, u32[]{:S(2)}) collective-permute-start(bf16[4,7168]{1,0:T(4,128)(2,1)S(1)} %get-tuple-element.40), channel_id=1, source_target_pairs={{0,8},{4,12},{8,0},{12,4},{1,9},{5,13},{9,1},{13,5},{2,10},{6,14},... | collective-permute-start | bytes 172040 | tf_op jit(solution)/shard_map/ppermute | solution.py:21
  41.5 6.1 %collective-permute-start.11 = (bf16[4,7168]{1,0:T(4,128)(2,1)S(1)}, bf16[4,7168]{1,0:T(4,128)(2,1)S(1)}, u32[]{:S(2)}, u32[]{:S(2)}) collective-permute-start(bf16[4,7168]{1,0:T(4,128)(2,1)S(1)} %get-tuple-element.39), channel_id=1, source_target_pairs={{0,12},{4,8},{8,4},{12,0},{1,13},{5,9},{9,5},{13,1},{2,14},{6,10},... | collective-permute-start | bytes 172040 | tf_op jit(solution)/shard_map/ppermute | solution.py:21
  42.9 4.8 %collective-permute-start.9 = (bf16[4,7168]{1,0:T(4,128)(2,1)S(1)}, bf16[4,7168]{1,0:T(4,128)(2,1)S(1)}, u32[]{:S(2)}, u32[]{:S(2)}) collective-permute-start(bf16[4,7168]{1,0:T(4,128)(2,1)S(1)} %get-tuple-element.38), channel_id=1, source_target_pairs={{0,4},{4,0},{8,12},{12,8},{1,5},{5,1},{9,13},{13,9},{2,6},{6,2},{1... | collective-permute-start | bytes 172040 | tf_op jit(solution)/shard_map/ppermute | solution.py:21

commit v5 on v4

--- a/solution.py
+++ b/solution.py
@@ -243,7 +243,7 @@
     count = tokens.shape[0]
     packed = pack(tokens, routes, gate_weights, experts_in.shape[0] * side)
     chunks = chunks_of(tokens.shape[1])[1]
-    last = 1 if chunks > 2 else 0
+    last = 2 if chunks > 2 else 0
     order = [*range(2, side), 1]
     along = [swap(packed, k, 0) for k in order]
     first = fetch(experts_in, 0, 0, chunks - last)

time: 48.5 us -> 48.5 us (level)
  waiting for transfers between devices: 8.67 us -> 9.59 us
  starting transfers between devices: 13.4 us -> 12.5 us
  transfers between devices with their start and end apart: 12 -> 12, of which waited for: 5 -> 7; matrix products, arithmetic and copies ran while one was open for 0% -> 0% of each run, Pallas kernels for 32% -> 32%
where the time goes in v5:
time: 48.5 us; the launch traced here: 48.4 us
  Pallas kernels  24.4 us (50%)
  starting transfers between devices  12.5 us (26%)
  waiting for transfers between devices  9.59 us (20%)
  other arithmetic  0.97 us (2%)
  between operations  0.79 us (2%)
    pallas_call x3, Pallas kernels, fetch(): pl.pallas_call(functools.partial(fetch_kernel, e, first), out_shape=pltpu...  11.6 us
    ppermute x6, starting transfers between devices, swap(): return lax.ppermute(x, 'side', [(i, i ^ side_bits) for i in range(side)])  9.45 us
    pallas_call x1, Pallas kernels, run_experts(): pl.pallas_call(functools.partial(experts_kernel, len(parts), tuple((len(x...  7.82 us
    ppermute x6, waiting for transfers between devices, swap(): return lax.ppermute(x, 'side', [(i, i ^ side_bits) for i in range(side)])  5.27 us
    ppermute x6, waiting for transfers between devices, swap(): return lax.ppermute(x, 'dev', [(i, i ^ dev_bits) for i in range(dev)])  4.32 us
    pallas_call x1, Pallas kernels, attend(): pl.pallas_call(attend_kernel, out_shape=pltpu.HBM(query_latent.shape, BF1...  4 us
    ppermute x6, starting transfers between devices, swap(): return lax.ppermute(x, 'dev', [(i, i ^ dev_bits) for i in range(dev)])  3.06 us
    pallas_call x1, Pallas kernels, pack(): pl.pallas_call(pack_kernel, out_shape=pltpu.VMEM((rows, width + pad), BF1...  1 us
  transfers between devices with their start and end apart: 12, of which 7 were waited for; matrix products, arithmetic and copies ran while one was open for 0% of the time, Pallas kernels for 32%

profile of v5, /device:TPU:0, one launch (start us, length us, event | category | flops | bytes accessed | tf_op | source)
XLA Modules:
  0.0 48.4 jit_solution(13831277010565173219)
XLA Ops:
  0.6 0.0 slice-start
  0.6 1.0 %pack.1 = bf16[4,7296]{1,0:T(4,128)(2,1)S(1)} custom-call(bf16[4,7168]{1,0:T(4,128)(2,1)} %tokens.1, s32[4,4]{1,0:T(4,128)} %routes.1, bf16[4,4]{1,0:T(4,128)(2,1)} %gates.1), custom_call_target="tpu_custom_call" | custom-call | tf_op jit(solution)/shard_map/pack/pallas_call | solution.py:60
  1.6 0.0 slice-start.1
  1.7 0.0 slice-start.2
  1.7 0.0 slice-start.3
  1.7 4.1 %collective-permute-start = (bf16[4,7296]{1,0:T(4,128)(2,1)S(1)}, bf16[4,7296]{1,0:T(4,128)(2,1)S(1)}, u32[]{:S(2)}, u32[]{:S(2)}) collective-permute-start(bf16[4,7296]{1,0:T(4,128)(2,1)S(1)} %pack.1), channel_id=1, source_target_pairs={{0,8},{4,12},{8,0},{12,4},{1,9},{5,13},{9,1},{13,5},{2,10},{6,14},... | collective-permute-start | bytes 175112 | tf_op jit(solution)/shard_map/ppermute | solution.py:21
  5.8 1.3 %collective-permute-start.1 = (bf16[4,7296]{1,0:T(4,128)(2,1)S(1)}, bf16[4,7296]{1,0:T(4,128)(2,1)S(1)}, u32[]{:S(2)}, u32[]{:S(2)}) collective-permute-start(bf16[4,7296]{1,0:T(4,128)(2,1)S(1)} %pack.1), channel_id=1, source_target_pairs={{0,12},{4,8},{8,4},{12,0},{1,13},{5,9},{9,5},{13,1},{2,14},{6,10},... | collective-permute-start | bytes 175112 | tf_op jit(solution)/shard_map/ppermute | solution.py:21
  7.1 0.2 collective-permute-start.2
  7.4 4.1 %fetch.3.refs_4_ = bf16[2,5120,512]{2,1,0:T(8,128)(2,1)S(1)} custom-call(bf16[2,2,7168,512]{3,2,1,0:T(8,128)(2,1)} %w_in.4), custom_call_target="tpu_custom_call" | custom-call | tf_op jit(solution)/shard_map/fetch/pallas_call | solution.py:95
  11.5 0.0 collective-permute-done
  11.5 0.4 collective-permute-done.1
  11.9 0.1 collective-permute-done.2
  11.9 0.1 pad_maximum_fusion.refs_0_
  12.1 1.6 %collective-permute-start.3 = (bf16[16,7296]{1,0:T(8,128)(2,1)S(1)}, bf16[16,7296]{1,0:T(8,128)(2,1)S(1)}, u32[]{:S(2)}, u32[]{:S(2)}) collective-permute-start(bf16[16,7296]{1,0:T(8,128)(2,1)S(1)} %pad_maximum_fusion.refs_0_), channel_id=1, source_target_pairs={{0,2},{1,3},{2,0},{3,1},{4,6},{5,7},{6,4},{7,5},{8,10},{9,11},{10,... | collective-permute-start | bytes 700424 | tf_op jit(solution)/shard_map/ppermute | solution.py:19
  13.6 0.0 slice-done
  13.7 0.0 slice-done.1
  13.7 0.0 slice-done.2
  13.7 0.0 slice-done.3
  13.7 5.3 %fetch.4.refs_6_ = bf16[2,7168,512]{2,1,0:T(8,128)(2,1)S(1)} custom-call(bf16[2,2,7168,512]{3,2,1,0:T(8,128)(2,1)} %w_in.4, bf16[2,512,7168]{2,1,0:T(8,128)(2,1)S(1)} %bitcast.1), custom_call_target="tpu_custom_call" | custom-call | tf_op jit(solution)/shard_map/fetch/pallas_call | solution.py:95
  19.0 0.1 collective-permute-start.4
  19.1 0.0 collective-permute-done.3.refs_1_
  19.1 0.5 %collective-permute-start.5 = (bf16[16,7296]{1,0:T(8,128)(2,1)S(1)}, bf16[16,7296]{1,0:T(8,128)(2,1)S(1)}, u32[]{:S(2)}, u32[]{:S(2)}) collective-permute-start(bf16[16,7296]{1,0:T(8,128)(2,1)S(1)} %collective-permute-done.3.refs_1_), channel_id=1, source_target_pairs={{0,1},{1,0},{2,3},{3,2},{4,5},{5,4},{6,7},{7,6},{8,9},{9,8},{10,11... | collective-permute-start | bytes 700424 | tf_op jit(solution)/shard_map/ppermute | solution.py:19
  19.6 2.2 %fetch.5.refs_5_ = bf16[2,2048,512]{2,1,0:T(8,128)(2,1)S(1)} custom-call(bf16[2,2,7168,512]{3,2,1,0:T(8,128)(2,1)} %w_in.4), custom_call_target="tpu_custom_call" | custom-call | tf_op jit(solution)/shard_map/fetch/pallas_call | solution.py:95
  21.8 0.0 collective-permute-done.4.refs_2_
  21.8 0.0 collective-permute-done.5.refs_3_
  21.8 7.8 %experts.1 = (bf16[16,7168]{1,0:T(8,128)(2,1)S(1)}, bf16[16,7168]{1,0:T(8,128)(2,1)S(1)}, bf16[16,7168]{1,0:T(8,128)(2,1)S(1)}, bf16[16,7168]{1,0:T(8,128)(2,1)S(1)}) custom-call(bf16[16,7296]{1,0:T(8,128)(2,1)S(1)} %pad_maximum_fusion.refs_0_, bf16[16,7296]{1,0:T(8,128)(2,1)S(1)} %collective-permute-done.3.refs_1_, ...), custom_call_target="tpu_custom_call" | custom-call | flops 2818572288 | bytes 44040192 | tf_op jit(solution)/shard_map/experts/pallas_call | solution.py:204
  29.6 0.2 collective-permute-start.6
  29.8 1.4 %collective-permute-done.6 = bf16[16,7168]{1,0:T(8,128)(2,1)S(1)} collective-permute-done((bf16[16,7168]{1,0:T(8,128)(2,1)S(1)}, bf16[16,7168]{1,0:T(8,128)(2,1)S(1)}, u32[]{:S(2)}, u32[]{:S(2)}) %collective-permute-start.6) | collective-permute-done | bytes 229408 | tf_op jit(solution)/shard_map/ppermute | solution.py:19
  31.2 0.1 add_convert_fusion.2
  31.3 0.7 %collective-permute-start.8 = (bf16[16,7168]{1,0:T(8,128)(2,1)S(1)}, bf16[16,7168]{1,0:T(8,128)(2,1)S(1)}, u32[]{:S(2)}, u32[]{:S(2)}) collective-permute-start(bf16[16,7168]{1,0:T(8,128)(2,1)S(1)} %add_convert_fusion.2), channel_id=1, source_target_pairs={{0,2},{1,3},{2,0},{3,1},{4,6},{5,7},{6,4},{7,5},{8,10},{9,11},{10,... | collective-permute-start | bytes 688136 | tf_op jit(solution)/shard_map/ppermute | solution.py:19
  32.0 0.1 collective-permute-start.7
  32.0 4.0 %attend.1 = bf16[2,128,512]{2,1,0:T(8,128)(2,1)} custom-call(s32[2]{0:T(128)} %lengths.1, bf16[2,128,512]{2,1,0:T(8,128)(2,1)} %queries.1, bf16[2,64,128]{2,1,0:T(8,128)(2,1)} %rope_queries.1, bf16[2,512,512]{2,1,0:T(8,128)(2,1)} %latents.1, bf16[2,64,512]{2,1,0:T(8,128)(2,1)} %ropes.1), custom_call_target="tpu_custom_call" | custom-call | tf_op jit(solution)/shard_map/attend/pallas_call | solution.py:139
  36.1 2.9 %collective-permute-done.8 = bf16[16,7168]{1,0:T(8,128)(2,1)S(1)} collective-permute-done((bf16[16,7168]{1,0:T(8,128)(2,1)S(1)}, bf16[16,7168]{1,0:T(8,128)(2,1)S(1)}, u32[]{:S(2)}, u32[]{:S(2)}) %collective-permute-start.8) | collective-permute-done | bytes 229408 | tf_op jit(solution)/shard_map/ppermute | solution.py:19
  39.0 0.0 collective-permute-done.7
  39.0 0.1 add_convert_fusion
  39.1 0.1 fusion
  39.1 2.4 %collective-permute-start.10 = (bf16[4,7168]{1,0:T(4,128)(2,1)S(1)}, bf16[4,7168]{1,0:T(4,128)(2,1)S(1)}, u32[]{:S(2)}, u32[]{:S(2)}) collective-permute-start(bf16[4,7168]{1,0:T(4,128)(2,1)S(1)} %get-tuple-element.40), channel_id=1, source_target_pairs={{0,8},{4,12},{8,0},{12,4},{1,9},{5,13},{9,1},{13,5},{2,10},{6,14},... | collective-permute-start | bytes 172040 | tf_op jit(solution)/shard_map/ppermute | solution.py:21
  41.6 1.3 %collective-permute-start.11 = (bf16[4,7168]{1,0:T(4,128)(2,1)S(1)}, bf16[4,7168]{1,0:T(4,128)(2,1)S(1)}, u32[]{:S(2)}, u32[]{:S(2)}) collective-permute-start(bf16[4,7168]{1,0:T(4,128)(2,1)S(1)} %get-tuple-element.39), channel_id=1, source_target_pairs={{0,12},{4,8},{8,4},{12,0},{1,13},{5,9},{9,5},{13,1},{2,14},{6,10},... | collective-permute-start | bytes 172040 | tf_op jit(solution)/shard_map/ppermute | solution.py:21
  42.9 0.0 collective-permute-start.9
  42.9 3.0 %collective-permute-done.10 = bf16[4,7168]{1,0:T(4,128)(2,1)S(1)} collective-permute-done((bf16[4,7168]{1,0:T(4,128)(2,1)S(1)}, bf16[4,7168]{1,0:T(4,128)(2,1)S(1)}, u32[]{:S(2)}, u32[]{:S(2)}) %collective-permute-start.10) | collective-permute-done | bytes 57376 | tf_op jit(solution)/shard_map/ppermute | solution.py:21
  45.9 1.8 %collective-permute-done.11 = bf16[4,7168]{1,0:T(4,128)(2,1)S(1)} collective-permute-done((bf16[4,7168]{1,0:T(4,128)(2,1)S(1)}, bf16[4,7168]{1,0:T(4,128)(2,1)S(1)}, u32[]{:S(2)}, u32[]{:S(2)}) %collective-permute-start.11) | collective-permute-done | bytes 57376 | tf_op jit(solution)/shard_map/ppermute | solution.py:21
  47.6 0.1 collective-permute-done.9
  47.7 0.7 %add_convert_fusion.3 = bf16[4,7168]{1,0:T(4,128)(2,1)} fusion(bf16[4,7168]{1,0:T(4,128)(2,1)S(1)} %collective-permute-done.11, bf16[4,7168]{1,0:T(4,128)(2,1)S(1)} %collective-permute-done.10, bf16[4,7168]{1,0:T(4,128)(2,1)S(1)} %collective-permute-done.9, bf16[16,7168]{1,0:T(8,128)(2,1)S(1)} %add_convert_fusion), kind=kLoop, calls=%fused_computation.4 | loop fusion | flops 229376 | bytes 286720 | tf_op jit(solution)/shard_map/convert_element_type | solution.py:226
  (1 shorter events, 0.0 us)
Async XLA Ops:
  0.6 13.0 %slice-start = ((s8[14680064]{0:T(1024)(128)(4,1)}), s8[4194304]{0:T(1024)(128)(4,1)S(1)}, s32[]{:S(2)}) async-start(s8[14680064]{0:T(1024)(128)(4,1)} %bitcast), calls=%async_computation | async-start | bytes 8388608
  1.6 12.0 %slice-start.1 = ((s8[14680064]{0:T(1024)(128)(4,1)}), s8[4194304]{0:T(1024)(128)(4,1)S(1)}, s32[]{:S(2)}) async-start(s8[14680064]{0:T(1024)(128)(4,1)} %bitcast), calls=%async_computation.1 | async-start | bytes 8388608
  1.7 12.0 %slice-start.2 = ((s8[14680064]{0:T(1024)(128)(4,1)}), s8[4194304]{0:T(1024)(128)(4,1)S(1)}, s32[]{:S(2)}) async-start(s8[14680064]{0:T(1024)(128)(4,1)} %bitcast), calls=%async_computation.2 | async-start | bytes 8388608
  1.7 12.0 %slice-start.3 = ((s8[14680064]{0:T(1024)(128)(4,1)}), s8[2097152]{0:T(1024)(128)(4,1)S(1)}, s32[]{:S(2)}) async-start(s8[14680064]{0:T(1024)(128)(4,1)} %bitcast), calls=%async_computation.3 | async-start | bytes 4194304
  1.7 9.8 %collective-permute-start = (bf16[4,7296]{1,0:T(4,128)(2,1)S(1)}, bf16[4,7296]{1,0:T(4,128)(2,1)S(1)}, u32[]{:S(2)}, u32[]{:S(2)}) collective-permute-start(bf16[4,7296]{1,0:T(4,128)(2,1)S(1)} %pack.1), channel_id=1, source_target_pairs={{0,8},{4,12},{8,0},{12,4},{1,9},{5,13},{9,1},{13,5},{2,10},{6,14},... | collective-permute-start | bytes 175112 | tf_op jit(solution)/shard_map/ppermute | solution.py:21
  5.8 6.1 %collective-permute-start.1 = (bf16[4,7296]{1,0:T(4,128)(2,1)S(1)}, bf16[4,7296]{1,0:T(4,128)(2,1)S(1)}, u32[]{:S(2)}, u32[]{:S(2)}) collective-permute-start(bf16[4,7296]{1,0:T(4,128)(2,1)S(1)} %pack.1), channel_id=1, source_target_pairs={{0,12},{4,8},{8,4},{12,0},{1,13},{5,9},{9,5},{13,1},{2,14},{6,10},... | collective-permute-start | bytes 175112 | tf_op jit(solution)/shard_map/ppermute | solution.py:21
  7.1 4.8 %collective-permute-start.2 = (bf16[4,7296]{1,0:T(4,128)(2,1)S(1)}, bf16[4,7296]{1,0:T(4,128)(2,1)S(1)}, u32[]{:S(2)}, u32[]{:S(2)}) collective-permute-start(bf16[4,7296]{1,0:T(4,128)(2,1)S(1)} %pack.1), channel_id=1, source_target_pairs={{0,4},{4,0},{8,12},{12,8},{1,5},{5,1},{9,13},{13,9},{2,6},{6,2},{1... | collective-permute-start | bytes 175112 | tf_op jit(solution)/shard_map/ppermute | solution.py:21
  12.1 7.0 %collective-permute-start.3 = (bf16[16,7296]{1,0:T(8,128)(2,1)S(1)}, bf16[16,7296]{1,0:T(8,128)(2,1)S(1)}, u32[]{:S(2)}, u32[]{:S(2)}) collective-permute-start(bf16[16,7296]{1,0:T(8,128)(2,1)S(1)} %pad_maximum_fusion.refs_0_), channel_id=1, source_target_pairs={{0,2},{1,3},{2,0},{3,1},{4,6},{5,7},{6,4},{7,5},{8,10},{9,11},{10,... | collective-permute-start | bytes 700424 | tf_op jit(solution)/shard_map/ppermute | solution.py:19
  19.0 2.8 %collective-permute-start.4 = (bf16[16,7296]{1,0:T(8,128)(2,1)S(1)}, bf16[16,7296]{1,0:T(8,128)(2,1)S(1)}, u32[]{:S(2)}, u32[]{:S(2)}) collective-permute-start(bf16[16,7296]{1,0:T(8,128)(2,1)S(1)} %pad_maximum_fusion.refs_0_), channel_id=1, source_target_pairs={{0,1},{1,0},{2,3},{3,2},{4,5},{5,4},{6,7},{7,6},{8,9},{9,8},{10,11... | collective-permute-start | bytes 700424 | tf_op jit(solution)/shard_map/ppermute | solution.py:19
  19.1 2.7 %collective-permute-start.5 = (bf16[16,7296]{1,0:T(8,128)(2,1)S(1)}, bf16[16,7296]{1,0:T(8,128)(2,1)S(1)}, u32[]{:S(2)}, u32[]{:S(2)}) collective-permute-start(bf16[16,7296]{1,0:T(8,128)(2,1)S(1)} %collective-permute-done.3.refs_1_), channel_id=1, source_target_pairs={{0,1},{1,0},{2,3},{3,2},{4,5},{5,4},{6,7},{7,6},{8,9},{9,8},{10,11... | collective-permute-start | bytes 700424 | tf_op jit(solution)/shard_map/ppermute | solution.py:19
  29.6 1.6 %collective-permute-start.6 = (bf16[16,7168]{1,0:T(8,128)(2,1)S(1)}, bf16[16,7168]{1,0:T(8,128)(2,1)S(1)}, u32[]{:S(2)}, u32[]{:S(2)}) collective-permute-start(bf16[16,7168]{1,0:T(8,128)(2,1)S(1)} %get-tuple-element.33), channel_id=1, source_target_pairs={{0,1},{1,0},{2,3},{3,2},{4,5},{5,4},{6,7},{7,6},{8,9},{9,8},{10,11... | collective-permute-start | bytes 688136 | tf_op jit(solution)/shard_map/ppermute | solution.py:19
  31.3 7.7 %collective-permute-start.8 = (bf16[16,7168]{1,0:T(8,128)(2,1)S(1)}, bf16[16,7168]{1,0:T(8,128)(2,1)S(1)}, u32[]{:S(2)}, u32[]{:S(2)}) collective-permute-start(bf16[16,7168]{1,0:T(8,128)(2,1)S(1)} %add_convert_fusion.2), channel_id=1, source_target_pairs={{0,2},{1,3},{2,0},{3,1},{4,6},{5,7},{6,4},{7,5},{8,10},{9,11},{10,... | collective-permute-start | bytes 688136 | tf_op jit(solution)/shard_map/ppermute | solution.py:19
  32.0 7.0 %collective-permute-start.7 = (bf16[16,7168]{1,0:T(8,128)(2,1)S(1)}, bf16[16,7168]{1,0:T(8,128)(2,1)S(1)}, u32[]{:S(2)}, u32[]{:S(2)}) collective-permute-start(bf16[16,7168]{1,0:T(8,128)(2,1)S(1)} %get-tuple-element.34), channel_id=1, source_target_pairs={{0,1},{1,0},{2,3},{3,2},{4,5},{5,4},{6,7},{7,6},{8,9},{9,8},{10,11... | collective-permute-start | bytes 688136 | tf_op jit(solution)/shard_map/ppermute | solution.py:19
  39.1 6.8 %collective-permute-start.10 = (bf16[4,7168]{1,0:T(4,128)(2,1)S(1)}, bf16[4,7168]{1,0:T(4,128)(2,1)S(1)}, u32[]{:S(2)}, u32[]{:S(2)}) collective-permute-start(bf16[4,7168]{1,0:T(4,128)(2,1)S(1)} %get-tuple-element.40), channel_id=1, source_target_pairs={{0,8},{4,12},{8,0},{12,4},{1,9},{5,13},{9,1},{13,5},{2,10},{6,14},... | collective-permute-start | bytes 172040 | tf_op jit(solution)/shard_map/ppermute | solution.py:21
  41.6 6.1 %collective-permute-start.11 = (bf16[4,7168]{1,0:T(4,128)(2,1)S(1)}, bf16[4,7168]{1,0:T(4,128)(2,1)S(1)}, u32[]{:S(2)}, u32[]{:S(2)}) collective-permute-start(bf16[4,7168]{1,0:T(4,128)(2,1)S(1)} %get-tuple-element.39), channel_id=1, source_target_pairs={{0,12},{4,8},{8,4},{12,0},{1,13},{5,9},{9,5},{13,1},{2,14},{6,10},... | collective-permute-start | bytes 172040 | tf_op jit(solution)/shard_map/ppermute | solution.py:21
  42.9 4.8 %collective-permute-start.9 = (bf16[4,7168]{1,0:T(4,128)(2,1)S(1)}, bf16[4,7168]{1,0:T(4,128)(2,1)S(1)}, u32[]{:S(2)}, u32[]{:S(2)}) collective-permute-start(bf16[4,7168]{1,0:T(4,128)(2,1)S(1)} %get-tuple-element.38), channel_id=1, source_target_pairs={{0,4},{4,0},{8,12},{12,8},{1,5},{5,1},{9,13},{13,9},{2,6},{6,2},{1... | collective-permute-start | bytes 172040 | tf_op jit(solution)/shard_map/ppermute | solution.py:21
